TPU v7x, 256 devices: a whole 4x4x8 slice. The times are simulated.
256 devices in a mesh: particle: 16 (over z, core), head: 16 (over x, y).
Axes of the slice: x: 4, y: 4, z: 8, core: 2. Of those that a mesh axis runs over, the one named last changes fastest.
Arguments:
- counts: int32 [128], P('particle'), may hold values from 0 to 8, as said below
- ssm_state: float32 [128, 128, 64, 128], P('particle', 'head'), may hold values from -6 to 6
- conv_value: float32 [128, 3, 8192], P('particle', None, 'head'), may hold values from -6 to 6
- conv_wread: float32 [128, 3, 1024], P('particle'), may hold values from -6 to 6
- token_ids: int32 [128, 4], replicated, may hold values from 0 to 65535
- embedding: bfloat16 [65536, 8192], P('head', 'particle'), may hold values from -6 to 6
- w_gate: bfloat16 [8192, 8192], P('particle', 'head'), may hold values from -0.0625 to 0.0625
- w_value: bfloat16 [8192, 8192], P('particle', 'head'), may hold values from -0.0625 to 0.0625
- w_wread: bfloat16 [8192, 1024], P('particle'), may hold values from -0.0625 to 0.0625
- w_step: bfloat16 [8192, 128], P('particle', 'head'), may hold values from -0.0625 to 0.0625
- kern_value: float32 [4, 8192], P(None, 'head'), may hold values from -0.5 to 0.5
- bias_value: float32 [8192], P('head'), may hold values from -0.5 to 0.5
- kern_wread: float32 [4, 1024], replicated, may hold values from -0.5 to 0.5
- bias_wread: float32 [1024], replicated, may hold values from -0.5 to 0.5
- step_bias: float32 [128], P('head'), may hold values from -4 to -1
- decay_log: float32 [128], P('head'), may hold values from 0 to 2.8
- skip_gain: float32 [128], P('head'), may hold values from 0.5 to 2
- norm_gain: float32 [8192], P('head'), may hold values from 0.5 to 1.5
- w_output: bfloat16 [8192, 8192], P('head', 'particle'), may hold values from -0.0625 to 0.0625
Outputs:
- mixed: bfloat16 [128, 4, 8192], P('head', None, 'particle')
- final_state: float32 [128, 128, 64, 128], P('particle', 'head')
- final_conv: float32 [128, 3, 8192], P('particle', None, 'head')
Inputs may be any that keep to these rules, and one draw needn't show every extreme that they name: counts sum to 128; the parent of child j lies between 8 * (j // 8) - 1 and 8 * (j // 8) + 6.
All inputs are finite; a program needn't handle non-finite values.
Results may differ from a plain program's by a relative error of at most 0.02.
Values may be sent and summed in bfloat16 or wider, within the bound.
A program may use at most 64 MiB of HBM per device.

v0:
```python
import math

import jax
import jax.numpy as jnp
from jax import lax
from jax.sharding import PartitionSpec as P

GROUPS = 4
INNER = 8192


EPSILON = 1e-05


def carried_in(part, axis, combine, identity):
    place = lax.axis_index(axis)
    gathered = jax.tree.map(lambda a: lax.all_gather(a, axis), part)
    state = jax.tree.map(lambda a, e: jnp.zeros_like(a) + jnp.asarray(e, a.dtype), part, identity)

    def one(step, state):
        return combine(
            state, jax.tree.map(lambda a: lax.dynamic_index_in_dim(a, step, 0, False), gathered)
        )

    return lax.fori_loop(0, place, one, state)


def from_behind(value, axis, steps):
    count = lax.axis_size(axis)
    initial, last = (max(0, -steps), min(count, count - steps))
    return lax.ppermute(value, axis, [(source, source + steps) for source in range(initial, last)])


def from_partner(array, axis, bit):
    return lax.ppermute(array, axis, [(i, i ^ 1 << bit) for i in range(lax.axis_size(axis))])


def pick_latest(earlier, latter):
    return (
        earlier[0] + latter[0],
        jnp.where(latter[2] > 0, latter[1], earlier[1]),
        jnp.maximum(earlier[2], latter[2]),
    )


def projector(tokens, weights):
    return jnp.concatenate(
        [jnp.dot(tokens, weight, preferred_element_type=jnp.float32) for weight in weights], axis=1
    )


def convolve(history, current, kernel, offset):
    window = jnp.concatenate([history, current[:, None, :].astype(jnp.float32)], axis=1)
    result = jax.nn.silu(jnp.sum(window * kernel[None], axis=1) + offset[None])
    return (result, window[:, 1:])


def on_device(
    counts,
    ssm_state,
    conv_value,
    conv_wread,
    token_ids,
    embedding,
    w_gate,
    w_value,
    w_wread,
    w_step,
    kern_value,
    bias_value,
    kern_wread,
    bias_wread,
    step_bias,
    decay_log,
    skip_gain,
    norm_gain,
    w_output,
):
    local_count = counts.shape[0]
    steps_count = token_ids.shape[1]
    own_rows = local_count * steps_count
    head_rank = lax.axis_index("head")
    part_rank = lax.axis_index("particle")
    head_devices = lax.axis_size("head")
    inner_local = w_gate.shape[1]
    heads_local = w_step.shape[1]
    wread_width = w_wread.shape[1]
    state_width = ssm_state.shape[3]
    vocab_rows = embedding.shape[0]
    shifted = token_ids.reshape(-1) - head_rank * vocab_rows
    inside = jnp.logical_and(shifted >= 0, shifted < vocab_rows)
    looked = jnp.take(embedding, jnp.clip(shifted, 0, vocab_rows - 1), axis=0)
    partial_rows = jnp.where(inside[:, None], looked.astype(jnp.float32), 0.0)
    tokens = lax.psum(partial_rows.astype(jnp.bfloat16), "head")
    summed = lax.psum_scatter(
        projector(tokens, (w_gate, w_value, w_step, w_wread)),
        "particle",
        scatter_dimension=0,
        tiled=True,
    )
    wread = summed[:, 2 * inner_local + heads_local :].astype(jnp.bfloat16)
    gate = (
        summed[:, :inner_local].astype(jnp.bfloat16).reshape(local_count, steps_count, inner_local)
    )
    value = (
        summed[:, inner_local : 2 * inner_local]
        .astype(jnp.bfloat16)
        .reshape(local_count, steps_count, inner_local)
    )
    rates = (
        summed[:, 2 * inner_local : 2 * inner_local + heads_local]
        .astype(jnp.bfloat16)
        .reshape(local_count, steps_count, heads_local)
    )
    wread = wread.reshape(local_count, steps_count, wread_width)
    children = part_rank * local_count + jnp.arange(local_count, dtype=jnp.int32)
    own_total = jnp.sum(counts)
    flag_one = jnp.ones((), jnp.int32)
    neutral = (jnp.zeros((), jnp.int32), jnp.zeros_like(counts), jnp.zeros((), jnp.int32))
    before, left_counts, left_flag = carried_in(
        (own_total, counts, flag_one), "particle", pick_latest, neutral
    )
    left_incl = before - jnp.sum(left_counts) + jnp.cumsum(left_counts)
    own_incl = before + jnp.cumsum(counts)
    window_incl = jnp.concatenate([left_incl, own_incl]).astype(jnp.int32)
    window_index = jnp.sum((window_incl[None, :] <= children[:, None]).astype(jnp.int32), axis=1)
    state_size = math.prod(ssm_state.shape[1:])
    value_size = math.prod(conv_value.shape[1:])
    packed = jnp.concatenate(
        [
            ssm_state.reshape(local_count, state_size),
            conv_value.reshape(local_count, value_size),
            conv_wread.reshape(local_count, -1),
        ],
        axis=1,
    )
    below = from_behind(packed.astype(jnp.bfloat16), "particle", 1).astype(packed.dtype)
    window = jnp.concatenate([below, packed], axis=0)
    chosen = jnp.take(window, window_index, axis=0)
    states = chosen[:, :state_size].reshape(ssm_state.shape)
    value_hist = chosen[:, state_size : state_size + value_size].reshape(conv_value.shape)
    wread_hist = chosen[:, state_size + value_size :].reshape(conv_wread.shape)
    group_span = head_devices // GROUPS
    group_rank = head_rank // group_span
    outputs = []
    for moment in range(steps_count):
        value_conv, value_hist = convolve(value_hist, value[:, moment], kern_value, bias_value)
        wread_conv, wread_hist = convolve(wread_hist, wread[:, moment], kern_wread, bias_wread)
        all_writes = wread_conv[:, : GROUPS * state_width].reshape(local_count, GROUPS, state_width)
        all_reads = wread_conv[:, GROUPS * state_width :].reshape(local_count, GROUPS, state_width)
        writes = lax.dynamic_index_in_dim(all_writes, group_rank, axis=1, keepdims=True)
        reads = lax.dynamic_index_in_dim(all_reads, group_rank, axis=1, keepdims=True)
        step_size = jax.nn.softplus(rates[:, moment].astype(jnp.float32) + step_bias[None])
        decay = jnp.exp(-step_size * jnp.exp(decay_log)[None])
        inputs = value_conv.reshape(local_count, heads_local, -1)
        states = (
            states * decay[:, :, None, None]
            + (step_size[:, :, None] * inputs)[:, :, :, None] * writes[:, :, None, :]
        )
        reading = jnp.sum(states * reads[:, :, None, :], axis=3) + skip_gain[None, :, None] * inputs
        outputs.append(reading.reshape(local_count, inner_local))
    mixer = jnp.stack(outputs, axis=1)
    gated = mixer * jax.nn.silu(gate.astype(jnp.float32))
    squares = jnp.sum(gated * gated, axis=2)
    for level in range(group_span.bit_length() - 1):
        squares = squares + from_partner(squares, "head", level)
    meansq = squares / (INNER // GROUPS)
    normed = (
        (gated * lax.rsqrt(meansq + EPSILON)[..., None] * norm_gain)
        .astype(jnp.bfloat16)
        .reshape(own_rows, inner_local)
    )
    every_row = lax.all_gather(normed, "particle", axis=0, tiled=True)
    out_rows = every_row.shape[0] // head_devices
    mixed = lax.psum_scatter(
        jnp.dot(every_row, w_output, preferred_element_type=jnp.float32).astype(jnp.bfloat16),
        "head",
        scatter_dimension=0,
        tiled=True,
    )
    mixed = mixed.reshape(out_rows // steps_count, steps_count, w_output.shape[1])
    return (mixed, states, value_hist)


def solution(mesh):
    return jax.shard_map(
        on_device,
        mesh=mesh,
        in_specs=(
            P("particle"),
            P("particle", "head", None, None),
            P("particle", None, "head"),
            P("particle", None, None),
            P(),
            P("head", "particle"),
            P("particle", "head"),
            P("particle", "head"),
            P("particle", None),
            P("particle", "head"),
            P(None, "head"),
            P("head"),
            P(),
            P(),
            P("head"),
            P("head"),
            P("head"),
            P("head"),
            P("head", "particle"),
        ),
        out_specs=(
            P("head", None, "particle"),
            P("particle", "head", None, None),
            P("particle", None, "head"),
        ),
        check_vma=False,
    )
```

profile of v0, /device:TPU:5, one launch (start us, length us, event | category | flops | bytes accessed | tf_op | source)
XLA Modules:
  0.0 322.2 jit_solution(7963934137163292286)
XLA Ops:
  9.3 4.7 %gather_fusion.1 = bf16[512,512]{1,0:T(8,128)(2,1)S(1)} fusion(bf16[4096,512]{1,0:T(8,128)(2,1)} %param.26, s32[1024]{0:T(1024)S(1)} %pad_clamp_fusion), kind=kCustom, calls=%fused_computation.1 | custom fusion | bytes 1050624 | tf_op jit(solution)/shard_map/jit(_take)/gather | solution.py:92
  15.1 2.8 copy.164
  19.2 4.1 %collective-permute-start = (bf16[8,70144]{1,0:T(8,128)(2,1)}, bf16[8,70144]{1,0:T(8,128)(2,1)}, u32[]{:S(2)}, u32[]{:S(2)}) collective-permute-start(bf16[8,70144]{1,0:T(8,128)(2,1)} %maximum_convert_fusion), channel_id=1, source_target_pairs={{0,16},{16,32},{32,48},{48,64},{64,80},{80,96},{96,112},{112,128},... | collective-permute-start | bytes 3366920 | tf_op jit(solution)/shard_map/ppermute | solution.py:31
  25.3 1.5 dynamic-update-slice
  27.8 15.0 %all-reduce.3 = (s32[16]{0:T(128)S(1)}, s32[16]{0:T(128)S(1)}, s32[128]{0:T(128)S(1)}) all-reduce(s32[16]{0:T(128)S(1)} %dynamic-update-slice, s32[16]{0:T(128)S(1)} %dynamic-update-slice.1, s32[128]{0:T(128)S(1)} %dynamic-update-slice.2), channel_id=1, replica_groups=mesh['particle'=16,'head'=16] {'particle'}, use_global_device_ids=true, to_apply=%add | all-reduce | flops 160 | bytes 1280
  42.8 2.7 while.14
  50.5 59.8 %all-reduce.6.cloned.1.call-done = bf16[512,512]{1,0:T(8,128)(2,1)} async-done(((bf16[512,512]{1,0:T(8,128)(2,1)}), bf16[512,512]{1,0:T(8,128)(2,1)}) %all-reduce.6.cloned.1.call-update) | async-done | bytes 524304 | tf_op jit(solution)/shard_map/psum | solution.py:94
  110.3 1.4 fusion.57
  111.7 2.6 fusion.55
  114.3 1.4 fusion.56
  115.7 2.0 fusion.58
  117.8 6.5 %concatenate.39 = f32[512,2056]{1,0:T(8,128)} concatenate(f32[512,512]{1,0:T(8,128)} %fusion.55, f32[512,512]{1,0:T(8,128)} %fusion.56, f32[512,8]{1,0:T(8,128)S(1)} %fusion.57, f32[512,1024]{1,0:T(8,128)} %fusion.58), dimensions={1} | concatenate | bytes 8421376 | tf_op jit(solution)/shard_map/concatenate | solution.py:47
  124.3 1.4 convert_element_type.113
  125.7 2.3 maximum_maximum_fusion
  128.1 4.6 %gather_fusion = f32[8,70144]{1,0:T(8,128)S(1)} fusion(f32[16,70144]{1,0:T(8,128)} %maximum_maximum_fusion, s32[1024]{0:T(1024)} %pad_clamp_fusion.1), kind=kCustom, calls=%fused_computation | custom fusion | bytes 4489248 | tf_op jit(solution)/shard_map/jit(_take)/gather | solution.py:139
  133.2 54.0 %reduce-scatter.3.cloned.1.call-done = f32[32,2056]{1,0:T(8,128)} async-done(((f32[512,2056]{1,0:T(8,128)}), f32[32,2056]{1,0:T(8,128)}) %reduce-scatter.3.cloned.1.call-update) | async-done | bytes 263184 | tf_op jit(solution)/shard_map/reduce_scatter | solution.py:95
  190.0 1.4 divide_multiply_fusion.3
  199.4 7.5 %multiply_reduce_fusion.2 = (f32[8,8,64]{2,1,0:T(8,128)}, f32[8,8,64]{2,1,0:T(8,128)}, f32[8,8,64]{2,1,0:T(8,128)}, f32[8,8,64]{2,1,0:T(8,128)S(1)}, f32[8,8,64,128]{3,2,1,0:T(8,128)}) fusion(f32[8,128]{1,0:T(8,128)} %dynamic-slice_bitcast_fusion.4, f32[8,128]{1,0:T(8,128)} %dynamic-slice_bitcast_fusion.5, f32[8,8,64]{2,1,0:T(8,128)S(1)} %get-tuple-element.129, ...), kind=kLoop, calls=%fused_computation.12 | loop fusion | flops 10469376 | bytes 4359168 | tf_op jit(solution)/shard_map/reduce_sum | solution.py:160
  209.8 1.3 collective-permute-start.1
  212.3 2.8 collective-permute-start.2
  217.1 21.7 %all_gather.23 = bf16[512,512]{1,0:T(8,128)(2,1)S(1)} all-gather(bf16[32,512]{1,0:T(8,128)(2,1)S(1)} %multiply_convert_fusion), channel_id=1, replica_groups=mesh['particle'=16,'head'=16] {'particle'}, dimensions={0}, use_global_device_ids=true | all-gather | bytes 557056 | tf_op jit(solution)/shard_map/all_gather | solution.py:173
  238.8 2.3 convolution_convert_fusion
  241.7 72.6 %reduce-scatter.5.cloned.1.call-done = bf16[32,512]{1,0:T(8,128)(2,1)} async-done(((bf16[512,512]{1,0:T(8,128)(2,1)}), bf16[32,512]{1,0:T(8,128)(2,1)}) %reduce-scatter.5.cloned.1.call-update) | async-done | bytes 32784 | tf_op jit(solution)/shard_map/reduce_scatter | solution.py:175
  314.3 1.4 reshape.833
  (133 shorter events, 30.2 us)
Async XLA Ops:
  7.2 108.6 %copy-start = (bf16[512,1024]{1,0:T(8,128)(2,1)S(1)}, bf16[512,1024]{1,0:T(8,128)(2,1)}, u32[]{:S(2)}) copy-start(bf16[512,1024]{1,0:T(8,128)(2,1)} %param.29) | copy-start | bytes 3145732
  7.2 103.1 %all-reduce.6.cloned.1.call-start = ((), (), s32[]{:S(2)}) async-start(), calls=%async_computation.2 | async-start | bytes 1048576 | tf_op jit(solution)/shard_map/psum | solution.py:94
  15.1 172.1 %reduce-scatter.3.cloned.1.call-start = ((), (), s32[]{:S(2)}) async-start(), calls=%async_computation.3 | async-start | bytes 4734976 | tf_op jit(solution)/shard_map/reduce_scatter | solution.py:95
  15.1 2.9 copy-start.3
  15.1 2.9 copy-start.4
  18.0 5.3 %copy-start.11 = (s32[8]{0:T(128)S(1)}, s32[8]{0:T(128)}, u32[]{:S(2)}) copy-start(s32[8]{0:T(128)} %param.21) | copy-start | bytes 100
  18.0 6.0 %copy-start.13 = (u32[256]{0:T(256)S(1)}, u32[256]{0:T(256)}, u32[]{:S(2)}) copy-start(u32[256]{0:T(256)} %constant.141) | copy-start | bytes 3076
  18.0 30.6 %copy-start.6 = (f32[512]{0:T(512)S(1)}, f32[512]{0:T(512)}, u32[]{:S(2)}) copy-start(f32[512]{0:T(512)} %param.32) | copy-start | bytes 6148
  18.0 31.3 %copy-start.12 = (f32[8]{0:T(128)S(1)}, f32[8]{0:T(128)}, u32[]{:S(2)}) copy-start(f32[8]{0:T(128)} %param.36) | copy-start | bytes 100
  18.0 31.8 %copy-start.10 = (f32[8]{0:T(128)S(1)}, f32[8]{0:T(128)}, u32[]{:S(2)}) copy-start(f32[8]{0:T(128)} %param.37) | copy-start | bytes 100
  19.2 105.2 %collective-permute-start = (bf16[8,70144]{1,0:T(8,128)(2,1)}, bf16[8,70144]{1,0:T(8,128)(2,1)}, u32[]{:S(2)}, u32[]{:S(2)}) collective-permute-start(bf16[8,70144]{1,0:T(8,128)(2,1)} %maximum_convert_fusion), channel_id=1, source_target_pairs={{0,16},{16,32},{32,48},{48,64},{64,80},{80,96},{96,112},{112,128},... | collective-permute-start | bytes 3366920 | tf_op jit(solution)/shard_map/ppermute | solution.py:31
  110.3 4.0 %copy-start.1 = (bf16[512,512]{1,0:T(8,128)(2,1)S(1)}, bf16[512,512]{1,0:T(8,128)(2,1)}, u32[]{:S(2)}) copy-start(bf16[512,512]{1,0:T(8,128)(2,1)} %all-reduce.6.cloned.1.call-done) | copy-start | bytes 1572868
  110.3 4.0 %copy-start.2 = (bf16[512,512]{1,0:T(8,128)(2,1)S(1)}, bf16[512,512]{1,0:T(8,128)(2,1)}, u32[]{:S(2)}) copy-start(bf16[512,512]{1,0:T(8,128)(2,1)} %param.28) | copy-start | bytes 1572868
  124.3 190.0 %reduce-scatter.5.cloned.1.call-start = ((), (), s32[]{:S(2)}) async-start(), calls=%async_computation.4 | async-start | bytes 557056 | tf_op jit(solution)/shard_map/reduce_scatter | solution.py:175
  128.1 4.7 %copy-start.9 = (pred[8]{0:T(512)(128)(4,1)S(1)}, pred[8]{0:T(512)(128)(4,1)}, u32[]{:S(2)}) copy-start(pred[8]{0:T(512)(128)(4,1)} %compare_and_fusion.2) | copy-start | bytes 28
  133.0 56.9 %copy-start.5 = (f32[4,1024]{1,0:T(4,128)S(1)}, f32[4,1024]{1,0:T(4,128)}, u32[]{:S(2)}) copy-start(f32[4,1024]{1,0:T(4,128)} %param.33) | copy-start | bytes 49156
  199.4 10.1 %copy-start.7 = (f32[512]{0:T(512)S(1)}, f32[512]{0:T(512)}, u32[]{:S(2)}) copy-start(f32[512]{0:T(512)} %param.32) | copy-start | bytes 6148
  199.4 10.0 %copy-start.8 = (f32[512]{0:T(512)S(1)}, f32[512]{0:T(512)}, u32[]{:S(2)}) copy-start(f32[512]{0:T(512)} %mul.477) | copy-start | bytes 6148
  209.8 2.5 collective-permute-start.1
  212.3 4.0 %collective-permute-start.2 = (f32[8,4]{1,0:T(8,128)S(1)}, f32[8,4]{1,0:T(8,128)S(1)}, u32[]{:S(2)}, u32[]{:S(2)}) collective-permute-start(f32[8,4]{1,0:T(8,128)S(1)} %add.520), channel_id=1, source_target_pairs={{0,2},{1,3},{2,0},{3,1},{4,6},{5,7},{6,4},{7,5},{8,10},{9,11},{10,... | collective-permute-start | bytes 392 | tf_op jit(solution)/shard_map/ppermute | solution.py:35
Sparse Core Ops, SparseCore 0:
  15.2 95.0 all-reduce.5
  124.4 62.6 reduce-scatter.2
  241.2 73.0 reduce-scatter.4
where the time goes:
time: 326 us; the launch traced here: 322 us
  waiting for transfers between devices  189 us (58%)
  local copies, waits for them, and re-layouts  37.3 us (11%)
  blocking collectives  36.7 us (11%)
  other arithmetic  24.5 us (8%)
  between operations  15.5 us (5%)
  matrix products  9.74 us (3%)
  starting transfers between devices  8.32 us (3%)
    reduce_scatter x1, waiting for transfers between devices, on_device(): lax.psum_scatter(jnp.dot(every_row, w_output, preferred_element_type=jnp....  72.6 us
    psum x1, waiting for transfers between devices, on_device(): tokens = lax.psum(partial_rows.astype(jnp.bfloat16), 'head')  59.8 us
    reduce_scatter x1, waiting for transfers between devices, on_device(): lax.psum_scatter(projector(tokens, (w_gate, w_value, w_step, w_wread)), '...  54 us
    all_gather x1, blocking collectives, on_device(): every_row = lax.all_gather(normed, 'particle', axis=0, tiled=True)  21.7 us
    unnamed x1, blocking collectives  15 us
    dot_general x4, matrix products, projector(): jnp.dot(tokens, weight, preferred_element_type=jnp.float32)  7.47 us
    reduce_sum x1, other arithmetic, on_device(): jnp.sum(states * reads[:, :, None, :], axis=3)  7.47 us
  transfers between devices with their start and end apart: 6, of which 5 were waited for; matrix products, arithmetic and copies ran while one was open for 11% of the time, Pallas kernels for 0%

commit v1 on v0

v1 whole, which is shorter than its diff:
```python
import functools

import jax
import jax.numpy as jnp
from jax import lax
from jax.experimental import pallas as pl
from jax.experimental.pallas import tpu as pltpu
from jax.sharding import PartitionSpec as P

GROUPS = 4
EPSILON = 1e-05
MESH = pl.DeviceIdType.MESH
F32 = jnp.float32
BF16 = jnp.bfloat16
LANES = 128
EMB_PIECES = 4


def silu(x):
    return x * (1.0 / (1.0 + jnp.exp(-x)))


def softplus(x):
    return jnp.maximum(x, 0.0) + jnp.log1p(jnp.exp(-jnp.abs(x)))


def iota(shape, axis):
    return lax.broadcasted_iota(jnp.int32, shape, axis)


def fused(
    np_,
    nh,
    counts,
    step_bias,
    decay_log,
    skip_gain,
    tok,
    kern_value,
    bias_value,
    kern_wread,
    bias_wread,
    norm_gain,
    ssm,
    conv_value,
    conv_wread,
    emb,
    w_gate,
    w_value,
    w_wread,
    w_step,
    w_output,
    mixed,
    final_state,
    final_conv,
    emb_v,
    wg_v,
    wv_v,
    ww_v,
    ws_v,
    wo_v,
    win,
    cwin,
    wwin,
    kw_v,
    sbf,
    fin,
    hist,
    whist,
    tok_part,
    tok_recv,
    tok_all,
    pv,
    pg,
    sv,
    sg,
    sendv_p,
    recvv_p,
    sendv_m,
    recvv_m,
    sendg_p,
    recvg_p,
    sendg_m,
    recvg_m,
    ss_own,
    ss_recv,
    nrm_all,
    part,
    part_recv,
    emb_sem,
    loc_sem,
    shift_send,
    shift_recv,
    rs_send,
    rs_recv,
    ag_send,
    ag_recv,
    sib_send,
    sib_recv,
    ring_send,
    ring_recv,
    ss_send,
    ss_rsem,
    nrm_send,
    nrm_recv,
    fwd_send,
    fwd_recv,
    out_send,
    out_recv,
    fin_sem,
):
    p = lax.axis_index("particle")
    h = lax.axis_index("head")
    zs = np_ // 2
    z = p // 2
    c = p % 2
    sibling = z * 2 + 1 - c
    kids = counts.shape[0]
    steps = tok.shape[1]
    own = kids * steps
    rows = np_ * own
    owned = rows // nh
    width = wv_v.shape[1]
    state = ssm.shape[3]
    heads = ssm.shape[1]
    headdim = ssm.shape[2]
    vocab = emb.shape[0]
    wide = width + 2 * state + LANES
    span = nh // GROUPS
    group = h // span

    barrier = pltpu.get_barrier_semaphore()

    def greet_head(j, _):
        pl.semaphore_signal(
            barrier, inc=1, device_id={"head": lax.rem(h + j, nh)}, device_id_type=MESH
        )
        return 0

    def greet_particle(j, _):
        pl.semaphore_signal(
            barrier, inc=1, device_id={"particle": lax.rem(p + j, np_)}, device_id_type=MESH
        )
        return 0

    lax.fori_loop(1, nh, greet_head, 0)
    lax.fori_loop(1, np_, greet_particle, 0)

    piece = vocab // EMB_PIECES
    emb_copies = [
        pltpu.make_async_copy(
            emb.at[pl.ds(i * piece, piece)], emb_v.at[pl.ds(i * piece, piece)], emb_sem.at[i]
        )
        for i in range(EMB_PIECES)
    ]
    for copy in emb_copies:
        copy.start()
    at_write = pl.ds(pl.multiple_of(group * state, state), state)
    at_read = pl.ds(pl.multiple_of((GROUPS + group) * state, state), state)
    lo, hi = pl.ds(0, state), pl.ds(state, state)
    pairs = [
        (ssm.at[pl.ds(0, kids - 1)], win.at[pl.ds(1, kids - 1)]),
        (conv_value.at[pl.ds(0, kids - 1)], cwin.at[pl.ds(1, kids - 1)]),
        (conv_wread.at[pl.ds(0, kids - 1), :, at_write], wwin.at[0, pl.ds(1, kids - 1)]),
        (conv_wread.at[pl.ds(0, kids - 1), :, at_read], wwin.at[1, pl.ds(1, kids - 1)]),
        (w_value, wv_v),
        (w_wread.at[:, at_write], ww_v.at[:, lo]),
        (w_wread.at[:, at_read], ww_v.at[:, hi]),
        (w_step, ws_v),
        (kern_wread.at[:, at_write], kw_v.at[:, lo]),
        (kern_wread.at[:, at_read], kw_v.at[:, hi]),
        (w_gate, wg_v),
        (w_output, wo_v),
    ]
    loads = [pltpu.make_async_copy(s, d, loc_sem.at[i]) for i, (s, d) in enumerate(pairs)]
    for copy in loads:
        copy.start()

    pl.semaphore_wait(barrier, nh - 1 + np_ - 1)

    above = lax.rem(p + 1, np_)
    shift_pairs = [
        (ssm.at[kids - 1], win.at[0]),
        (conv_value.at[kids - 1], cwin.at[0]),
        (conv_wread.at[kids - 1, :, at_write], wwin.at[0, 0]),
        (conv_wread.at[kids - 1, :, at_read], wwin.at[1, 0]),
    ]
    shifts = [
        pltpu.make_async_remote_copy(
            src_ref=s,
            dst_ref=d,
            send_sem=shift_send.at[i],
            recv_sem=shift_recv.at[i],
            device_id={"particle": above},
            device_id_type=MESH,
        )
        for i, (s, d) in enumerate(shift_pairs)
    ]
    for copy in shifts:
        copy.start()

    column = jnp.concatenate(
        [
            tok[b * kids : (b + 1) * kids, t : t + 1]
            for b in range(np_)
            for t in range(steps)
        ],
        axis=0,
    ) - h * vocab
    half, half_h = rows // 2, nh // 2

    def rs_copy(dest):
        return pltpu.make_async_remote_copy(
            src_ref=tok_part.at[dest],
            dst_ref=tok_recv.at[h],
            send_sem=rs_send.at[dest],
            recv_sem=rs_recv.at[h],
            device_id={"head": dest},
            device_id_type=MESH,
        )

    for m in range(2):
        ids = column[m * half : (m + 1) * half]
        total = None
        for i in range(EMB_PIECES):
            if m == 0:
                emb_copies[i].wait()
            hot = jnp.where(ids - i * piece == iota((half, piece), 1), 1.0, 0.0).astype(BF16)
            term = jnp.dot(hot, emb_v[pl.ds(i * piece, piece)], preferred_element_type=F32)
            total = term if total is None else total + term
        tok_part[pl.ds(m * half_h, half_h)] = total.astype(BF16).reshape(half_h, owned, -1)

        def send_rows(j, _, m=m):
            dest = m * half_h + lax.rem(h + j, half_h)

            @pl.when(dest != h)
            def _():
                rs_copy(dest).start()

            return 0

        lax.fori_loop(0, half_h, send_rows, 0)

    counted = counts[0]
    for i in range(1, kids - 1):
        counted = counted + counts[i]
    running = kids - counted
    marks = [running]
    for i in range(kids - 2):
        running = running + counts[i]
        marks.append(running)
    marks.append(running + counts[kids - 2])
    parent = []
    for k in range(kids):
        at = jnp.int32(0)
        for mark in marks:
            at = at + (mark <= k).astype(jnp.int32)
        parent.append(jnp.minimum(at, kids - 1))
    for copy in loads[:4]:
        copy.wait()
    for copy in shifts:
        copy.wait_recv()
    for k in range(kids):
        sbf[:, pl.ds(k * state, state)] = win[parent[k]].reshape(width, state).astype(BF16)
        picked = cwin[parent[k]]
        for tap in range(3):
            hist[tap, pl.ds(k, 1), :] = picked[tap : tap + 1]
        for side in range(2):
            picked = wwin[side, parent[k]]
            for tap in range(3):
                whist[tap, pl.ds(k, 1), pl.ds(side * state, state)] = picked[tap : tap + 1]

    def rs_wait(s, _):
        @pl.when(s != h)
        def _():
            pltpu.make_async_remote_copy(
                src_ref=tok_part.at[s],
                dst_ref=tok_recv.at[s],
                send_sem=rs_send.at[s],
                recv_sem=rs_recv.at[s],
                device_id={"head": s},
                device_id_type=MESH,
            ).wait()

        return 0

    tok_recv[h] = tok_part[h]
    lax.fori_loop(0, nh, rs_wait, 0)
    shared = tok_recv[0]
    for s in range(1, nh):
        shared = shared + tok_recv[s]
    tok_all[h] = shared

    def ag_copy(j, slot):
        return pltpu.make_async_remote_copy(
            src_ref=tok_all.at[h],
            dst_ref=tok_all.at[h],
            send_sem=ag_send.at[slot],
            recv_sem=ag_recv.at[slot],
            device_id={"head": lax.rem(h + j, nh)},
            device_id_type=MESH,
        )

    def ag_start(j, _):
        ag_copy(j, j).start()
        return 0

    def ag_wait(j, _):
        source = lax.rem(h + nh - j, nh)
        pltpu.make_async_remote_copy(
            src_ref=tok_all.at[h],
            dst_ref=tok_all.at[source],
            send_sem=ag_send.at[j],
            recv_sem=ag_recv.at[j],
            device_id={"head": source},
            device_id_type=MESH,
        ).wait()
        return 0

    lax.fori_loop(1, nh, ag_start, 0)
    for copy in loads[4:]:
        copy.wait()
    lax.fori_loop(1, nh, ag_wait, 0)

    tokens = tok_all[...].reshape(rows, -1)
    reach = zs // 2
    order = [reach]
    for d in range(reach - 1, 0, -1):
        order += [d, -d]
    order.append(0)

    def chip(d):
        return lax.rem(z + d + zs, zs)

    def sib_copy(source, target, kind, i):
        at = chip(order[i])
        return pltpu.make_async_remote_copy(
            src_ref=source.at[1 - c, at],
            dst_ref=target.at[at],
            send_sem=sib_send.at[kind, i],
            recv_sem=sib_recv.at[kind, i],
            device_id={"particle": sibling},
            device_id_type=MESH,
        )

    value_part = jnp.dot(tokens, wv_v[...], preferred_element_type=F32).astype(BF16)
    wread_part = jnp.dot(tokens, ww_v[...], preferred_element_type=F32).astype(BF16)
    step_part = jnp.dot(tokens, ws_v[...], preferred_element_type=F32).astype(BF16)
    rest = jnp.zeros((rows, LANES - heads), BF16)
    step_part = jnp.concatenate([step_part, rest], axis=1)
    for b in range(np_):
        at = slice(b * own, (b + 1) * own)
        pv[b % 2, b // 2, :, pl.ds(0, width)] = value_part[at]
        pv[b % 2, b // 2, :, pl.ds(width, 2 * state)] = wread_part[at]
        pv[b % 2, b // 2, :, pl.ds(width + 2 * state, LANES)] = step_part[at]
    for i in range(zs):
        sib_copy(pv, sv, 0, i).start()
    gate_part = jnp.dot(tokens, wg_v[...], preferred_element_type=F32).astype(BF16)
    for b in range(np_):
        pg[b % 2, b // 2] = gate_part[b * own : (b + 1) * own]
    for i in range(zs):
        sib_copy(pg, sg, 1, i).start()

    arrived = set()

    def chip_sum(kind, d):
        d = d if d != -reach else reach
        i = order.index(d)
        source, target = ((pv, sv), (pg, sg))[kind]
        if (kind, i) not in arrived:
            arrived.add((kind, i))
            sib_copy(source, target, kind, i).wait_recv()
        at = chip(d)
        return source[c, at].astype(F32) + target[at].astype(F32)

    streams = [
        (0, 1, reach, sendv_p, recvv_p),
        (0, -1, reach - 1, sendv_m, recvv_m),
        (1, 1, reach - 1, sendg_p, recvg_p),
        (1, -1, reach, sendg_m, recvg_m),
    ]

    def ring_copy(n, s):
        _, way, _, out, back = streams[n]
        return pltpu.make_async_remote_copy(
            src_ref=out.at[s],
            dst_ref=back.at[s],
            send_sem=ring_send.at[n, s],
            recv_sem=ring_recv.at[n, s],
            device_id={"particle": lax.rem(p + 2 * way + np_, np_)},
            device_id_type=MESH,
        )

    for s in range(reach):
        for n, (kind, way, hops, out, back) in enumerate(streams):
            if s >= hops:
                continue
            term = chip_sum(kind, way * (hops - s))
            if s > 0:
                ring_copy(n, s - 1).wait_recv()
                term = term + back[s - 1].astype(F32)
            out[s] = term.astype(BF16)
            ring_copy(n, s).start()

    def ring_total(kind):
        term = chip_sum(kind, 0)
        for n in (2 * kind, 2 * kind + 1):
            hops, back = streams[n][2], streams[n][4]
            if hops > 0:
                ring_copy(n, hops - 1).wait_recv()
                term = term + back[hops - 1].astype(F32)
        return term.astype(BF16)

    summed = ring_total(0)

    def at_step(a, t):
        return a[t * kids : (t + 1) * kids]

    value = summed[:, :width].astype(F32)
    wread = summed[:, width : width + 2 * state].astype(F32)
    spread = (iota((LANES, width), 1) // headdim == iota((LANES, width), 0)).astype(F32)
    rates = jnp.dot(
        summed[:, width + 2 * state :], spread.astype(BF16), preferred_element_type=F32
    )
    lane_head = iota((1, width), 1) // headdim

    def per_head(ref):
        out = jnp.zeros((1, width), F32)
        for i in range(heads):
            out = jnp.where(lane_head == i, ref[i], out)
        return out

    step_size = softplus(rates + per_head(step_bias))
    decay = jnp.exp(-step_size * jnp.exp(per_head(decay_log)))
    skip = per_head(skip_gain)
    kern = kern_value[...]
    kern_w = kw_v[...]
    bias = bias_value[...]
    bias_w = jnp.concatenate([bias_wread[:, at_write], bias_wread[:, at_read]], axis=1)
    seq = [hist[i] for i in range(3)] + [at_step(value, t) for t in range(steps)]
    seq_w = [whist[i] for i in range(3)] + [at_step(wread, t) for t in range(steps)]
    conv, conv_w = [], []
    for t in range(steps):
        a, b = seq[t] * kern[0:1], seq_w[t] * kern_w[0:1]
        for i in range(1, 4):
            a = a + seq[t + i] * kern[i : i + 1]
            b = b + seq_w[t + i] * kern_w[i : i + 1]
        conv.append(silu(a + bias))
        conv_w.append(silu(b + bias_w))
    writes = [a[:, :state] for a in conv_w]
    reads = [a[:, state:] for a in conv_w]

    child = iota((own, state), 0) % kids

    def apart(blocks):
        whole = jnp.concatenate(blocks, axis=0)
        return jnp.concatenate(
            [jnp.where(child == k, whole, 0.0) for k in range(kids)], axis=1
        ).astype(BF16)

    first = lax.dot_general(
        apart(reads), sbf[...], (((1,), (1,)), ((), ())), preferred_element_type=F32
    )
    kept = None
    added = []
    readings = []
    for t in range(steps):
        now = at_step(decay, t)
        kept = now if kept is None else kept * now
        added = [a * now for a in added] + [at_step(step_size, t) * conv[t]]
        reading = kept * at_step(first, t) + skip * conv[t]
        for u in range(t + 1):
            match = jnp.sum(writes[u] * reads[t], axis=1, keepdims=True)
            reading = reading + added[u] * match
        readings.append(reading)
    gate = ring_total(1).astype(F32)
    gated = jnp.concatenate(readings, axis=0) * silu(gate)

    squares = jnp.sum(gated * gated, axis=1, keepdims=True)
    ss_own[...] = jnp.broadcast_to(squares, (own, LANES))

    def ss_copy(j):
        mate = group * span + lax.rem(h + j, span)
        return pltpu.make_async_remote_copy(
            src_ref=ss_own,
            dst_ref=ss_recv.at[j - 1],
            send_sem=ss_send.at[j - 1],
            recv_sem=ss_rsem.at[j - 1],
            device_id={"head": mate},
            device_id_type=MESH,
        )

    for j in range(1, span):
        ss_copy(j).start()
    meansq = ss_own[...]
    for j in range(1, span):
        ss_copy(j).wait_recv()
        meansq = meansq + ss_recv[j - 1]
    scale = lax.rsqrt(meansq[:, :1] / (width * span) + EPSILON)
    normed = (gated * scale * norm_gain[...]).astype(BF16)
    at_row, from_row = iota((own, own), 0), iota((own, own), 1)
    turn = (from_row == (at_row % steps) * kids + at_row // steps).astype(F32).astype(BF16)
    nrm_all[p] = jnp.dot(turn, normed, preferred_element_type=F32).astype(BF16)

    def nrm_copy(at, target, send, recv):
        return pltpu.make_async_remote_copy(
            src_ref=nrm_all.at[at],
            dst_ref=nrm_all.at[at],
            send_sem=send,
            recv_sem=recv,
            device_id={"particle": target},
            device_id_type=MESH,
        )

    def direct(j):
        return nrm_copy(p, lax.rem(p + 2 * j, np_), nrm_send.at[j - 1], nrm_recv.at[j - 1])

    def forward(j):
        at = lax.rem(p + np_ - 2 * j, np_)
        return nrm_copy(at, sibling, fwd_send.at[j], fwd_recv.at[j])

    near = []
    for d in range(1, reach):
        near += [d, zs - d]
    near.append(reach)
    for j in reversed(near):
        direct(j).start()
    forward(0).start()

    adds = lax.dot_general(
        jnp.concatenate(added, axis=0).astype(BF16),
        apart(writes),
        (((0,), (0,)), ((), ())),
        preferred_element_type=F32,
    )
    for k in range(kids):
        for i in range(heads):
            factor = jnp.broadcast_to(
                kept[k : k + 1, i * headdim : i * headdim + 1], (headdim, state)
            )
            fin[k, i] = (
                win[parent[k], i] * factor
                + adds[i * headdim : (i + 1) * headdim, k * state : (k + 1) * state]
            )
    finals = pltpu.make_async_copy(fin, final_state, fin_sem)
    finals.start()
    for i in range(3):
        final_conv[:, i, :] = at_step(value, steps - 3 + i)

    for j in near:
        at = lax.rem(p + np_ - 2 * j, np_)
        nrm_copy(at, sibling, nrm_send.at[j - 1], nrm_recv.at[j - 1]).wait_recv()
        forward(j).start()
    for j in range(zs):
        at = lax.rem(sibling + np_ - 2 * j, np_)
        nrm_copy(at, sibling, fwd_send.at[j], fwd_recv.at[j]).wait_recv()

    product = jnp.dot(
        nrm_all[...].reshape(rows, width), wo_v[...], preferred_element_type=F32
    ).astype(BF16)
    part[...] = product.reshape(nh, owned, -1)

    def out_copy(j):
        dest = lax.rem(h + j, nh)
        return pltpu.make_async_remote_copy(
            src_ref=part.at[dest],
            dst_ref=part_recv.at[j - 1],
            send_sem=out_send.at[j - 1],
            recv_sem=out_recv.at[j - 1],
            device_id={"head": dest},
            device_id_type=MESH,
        )

    def out_start(j, _):
        out_copy(j).start()
        return 0

    def out_wait(j, _):
        out_copy(j).wait()
        return 0

    lax.fori_loop(1, nh, out_start, 0)

    for copy in shifts:
        copy.wait_send()
    for kind, (source, target) in enumerate(((pv, sv), (pg, sg))):
        for i in range(zs):
            sib_copy(source, target, kind, i).wait_send()
    for n in range(4):
        for s in range(streams[n][2]):
            ring_copy(n, s).wait_send()
    for j in range(1, span):
        ss_copy(j).wait_send()
    for j in range(1, zs):
        direct(j).wait_send()
    for j in range(zs):
        forward(j).wait_send()

    lax.fori_loop(1, nh, out_wait, 0)
    answer = part[h].astype(F32)
    for j in range(nh - 1):
        answer = answer + part_recv[j].astype(F32)
    mixed[...] = answer.reshape(mixed.shape).astype(BF16)
    finals.wait()


def on_device(
    np_,
    nh,
    counts,
    ssm_state,
    conv_value,
    conv_wread,
    token_ids,
    embedding,
    w_gate,
    w_value,
    w_wread,
    w_step,
    kern_value,
    bias_value,
    kern_wread,
    bias_wread,
    step_bias,
    decay_log,
    skip_gain,
    norm_gain,
    w_output,
):
    kids, heads, headdim, state = ssm_state.shape
    steps = token_ids.shape[1]
    own = kids * steps
    rows = np_ * own
    owned = rows // nh
    depth, width = w_value.shape
    cols = w_output.shape[1]
    zs = np_ // 2
    reach = zs // 2
    wide = width + 2 * state + LANES
    span = nh // GROUPS
    taps = kern_value.shape[0]
    back = max(reach - 1, 1)
    dma = pltpu.SemaphoreType.DMA
    scratch = [
        pltpu.VMEM(embedding.shape, BF16),
        pltpu.VMEM((depth, width), BF16),
        pltpu.VMEM((depth, width), BF16),
        pltpu.VMEM((depth, 2 * state), BF16),
        pltpu.VMEM((depth, heads), BF16),
        pltpu.VMEM((width, cols), BF16),
        pltpu.VMEM((kids, heads, headdim, state), F32),
        pltpu.VMEM((kids, 3, width), F32),
        pltpu.VMEM((2, kids, 3, state), F32),
        pltpu.VMEM((taps, 2 * state), F32),
        pltpu.VMEM((width, kids * state), BF16),
        pltpu.VMEM((kids, heads, headdim, state), F32),
        pltpu.VMEM((3, kids, width), F32),
        pltpu.VMEM((3, kids, 2 * state), F32),
        pltpu.VMEM((nh, owned, depth), BF16),
        pltpu.VMEM((nh, owned, depth), BF16),
        pltpu.VMEM((nh, owned, depth), BF16),
        pltpu.VMEM((2, zs, own, wide), BF16),
        pltpu.VMEM((2, zs, own, width), BF16),
        pltpu.VMEM((zs, own, wide), BF16),
        pltpu.VMEM((zs, own, width), BF16),
        pltpu.VMEM((reach, own, wide), BF16),
        pltpu.VMEM((reach, own, wide), BF16),
        pltpu.VMEM((back, own, wide), BF16),
        pltpu.VMEM((back, own, wide), BF16),
        pltpu.VMEM((back, own, width), BF16),
        pltpu.VMEM((back, own, width), BF16),
        pltpu.VMEM((reach, own, width), BF16),
        pltpu.VMEM((reach, own, width), BF16),
        pltpu.VMEM((own, LANES), F32),
        pltpu.VMEM((span - 1, own, LANES), F32),
        pltpu.VMEM((np_, own, width), BF16),
        pltpu.VMEM((nh, owned, cols), BF16),
        pltpu.VMEM((nh - 1, owned, cols), BF16),
        dma((EMB_PIECES,)),
        dma((12,)),
        dma((4,)),
        dma((4,)),
        dma((nh,)),
        dma((nh,)),
        dma((nh,)),
        dma((nh,)),
        dma((2, zs)),
        dma((2, zs)),
        dma((4, reach)),
        dma((4, reach)),
        dma((span - 1,)),
        dma((span - 1,)),
        dma((zs - 1,)),
        dma((zs - 1,)),
        dma((zs,)),
        dma((zs,)),
        dma((nh - 1,)),
        dma((nh - 1,)),
        dma,
    ]
    smem = pl.BlockSpec(memory_space=pltpu.SMEM)
    vmem = pl.BlockSpec(memory_space=pltpu.VMEM)
    hbm = pl.BlockSpec(memory_space=pl.ANY)
    return pl.pallas_call(
        functools.partial(fused, np_, nh),
        out_shape=(
            jax.ShapeDtypeStruct((owned // steps, steps, cols), BF16),
            jax.ShapeDtypeStruct(ssm_state.shape, F32),
            jax.ShapeDtypeStruct(conv_value.shape, F32),
        ),
        in_specs=[smem] * 4 + [vmem] * 3 + [hbm] + [vmem] * 2 + [hbm] * 9,
        out_specs=(vmem, hbm, vmem),
        scratch_shapes=scratch,
        compiler_params=pltpu.CompilerParams(
            collective_id=0, has_side_effects=True, vmem_limit_bytes=48 * 1024 * 1024
        ),
    )(
        counts,
        step_bias,
        decay_log,
        skip_gain,
        token_ids,
        kern_value,
        bias_value.reshape(1, -1),
        kern_wread,
        bias_wread.reshape(1, -1),
        norm_gain.reshape(1, -1),
        ssm_state,
        conv_value,
        conv_wread,
        embedding,
        w_gate,
        w_value,
        w_wread,
        w_step,
        w_output,
    )


def solution(mesh):
    return jax.shard_map(
        functools.partial(on_device, mesh.shape["particle"], mesh.shape["head"]),
        mesh=mesh,
        in_specs=(
            P("particle"),
            P("particle", "head", None, None),
            P("particle", None, "head"),
            P("particle", None, None),
            P(),
            P("head", "particle"),
            P("particle", "head"),
            P("particle", "head"),
            P("particle", None),
            P("particle", "head"),
            P(None, "head"),
            P("head"),
            P(),
            P(),
            P("head"),
            P("head"),
            P("head"),
            P("head"),
            P("head", "particle"),
        ),
        out_specs=(
            P("head", None, "particle"),
            P("particle", "head", None, None),
            P("particle", None, "head"),
        ),
        check_vma=False,
    )
```

time: 326 us -> 87.7 us (0.27)
  the two profiles are of different devices: /device:TPU:5 before, /device:TPU:1 now
where the time goes in v1:
time: 87.7 us; the launch traced here: 87.1 us
  Pallas kernels  70 us (80%)
  local copies, waits for them, and re-layouts  16.4 us (19%)
    pallas_call x1, Pallas kernels, on_device(): pl.pallas_call(functools.partial(fused, np_, nh), out_shape=(jax.ShapeDty...  70 us
    unnamed x32, local copies, waits for them, and re-layouts  15.8 us

profile of v1, /device:TPU:1, one launch (start us, length us, event | category | flops | bytes accessed | tf_op | source)
XLA Modules:
  0.0 87.1 jit_solution(14455411795680567877)
XLA Ops:
  0.6 0.8 copy.23.conv_value
  1.5 0.8 copy.22.tok
  2.3 1.0 %copy.24.conv_wread = f32[8,3,1024]{2,1,0:T(4,128)S(1)} copy(f32[8,3,1024]{2,0,1:T(8,128)} %param.22) | data formatting | bytes 196608 | tf_op args[3]
  3.2 0.9 copy.25.w_step
  4.1 0.0 copy-start
  4.1 1.2 %copy-done = bf16[512,1024]{1,0:T(8,128)(2,1)S(1)} copy-done((bf16[512,1024]{1,0:T(8,128)(2,1)S(1)}, bf16[512,1024]{1,0:T(8,128)(2,1)}, u32[]{:S(2)}) %copy-start) | copy-done | bytes 1048600
  5.3 1.0 %copy-done.1 = bf16[512,512]{1,0:T(8,128)(2,1)S(1)} copy-done((bf16[512,512]{1,0:T(8,128)(2,1)S(1)}, bf16[512,512]{1,0:T(8,128)(2,1)}, u32[]{:S(2)}) %copy-start.1) | copy-done | bytes 524312
  6.4 0.0 copy-start.2
  6.4 1.0 %copy-done.2 = bf16[512,512]{1,0:T(8,128)(2,1)S(1)} copy-done((bf16[512,512]{1,0:T(8,128)(2,1)S(1)}, bf16[512,512]{1,0:T(8,128)(2,1)}, u32[]{:S(2)}) %copy-start.2) | copy-done | bytes 524312
  7.4 0.0 copy-start.3
  7.4 1.0 %copy-done.3 = bf16[512,512]{1,0:T(8,128)(2,1)S(1)} copy-done((bf16[512,512]{1,0:T(8,128)(2,1)S(1)}, bf16[512,512]{1,0:T(8,128)(2,1)}, u32[]{:S(2)}) %copy-start.3) | copy-done | bytes 524312
  8.4 0.7 copy-done.4
  9.2 0.7 copy-done.5
  9.9 0.7 copy-done.6
  10.5 0.7 copy-done.7
  11.2 0.7 copy-done.8
  11.9 0.7 copy-done.9
  12.6 0.7 copy-done.10
  13.2 0.7 copy-done.11
  13.9 0.7 copy-done.12
  14.5 70.0 %shard_map.202 = (bf16[8,4,512]{2,1,0:T(4,128)(2,1)S(1)}, f32[8,8,64,128]{3,2,1,0:T(8,128)S(1)}, f32[8,3,512]{2,1,0:T(4,128)S(1)}) custom-call(s32[8]{0:T(128)S(1)} %copy-done.9, f32[8]{0:T(128)S(1)} %copy-done.10, f32[8]{0:T(128)S(1)} %copy-done.11, f32[8]{0:T(128)S(1)} %copy-done.12, s32[128,4]{1,0:T(8,128)S(1)} %copy.22.tok, f32[4,512]{1,0:T(4,128)S(1)} %copy-done.5, ...), custom_call_target="tpu_custom_call" | custom-call | tf_op jit(solution)/shard_map/pallas_call | solution.py:704
  84.5 0.6 copy.26
  85.1 0.6 copy.29
  85.8 1.3 %copy.30 = f32[8,8,64,128]{3,2,1,0:T(8,128)} copy(f32[8,8,64,128]{3,2,1,0:T(8,128)S(1)} %get-tuple-element.10) | data formatting | bytes 4194304
  (10 shorter events, 0.0 us)
Async XLA Ops:
  4.1 1.2 %copy-start = (bf16[512,1024]{1,0:T(8,128)(2,1)S(1)}, bf16[512,1024]{1,0:T(8,128)(2,1)}, u32[]{:S(2)}) copy-start(bf16[512,1024]{1,0:T(8,128)(2,1)} %w_wread.1) | copy-start | bytes 3145732
  5.3 1.0 %copy-start.1 = (bf16[512,512]{1,0:T(8,128)(2,1)S(1)}, bf16[512,512]{1,0:T(8,128)(2,1)}, u32[]{:S(2)}) copy-start(bf16[512,512]{1,0:T(8,128)(2,1)} %w_gate.1) | copy-start | bytes 1572868
  6.4 1.0 %copy-start.2 = (bf16[512,512]{1,0:T(8,128)(2,1)S(1)}, bf16[512,512]{1,0:T(8,128)(2,1)}, u32[]{:S(2)}) copy-start(bf16[512,512]{1,0:T(8,128)(2,1)} %w_value.1) | copy-start | bytes 1572868
  7.4 1.0 %copy-start.3 = (bf16[512,512]{1,0:T(8,128)(2,1)S(1)}, bf16[512,512]{1,0:T(8,128)(2,1)}, u32[]{:S(2)}) copy-start(bf16[512,512]{1,0:T(8,128)(2,1)} %w_output.1) | copy-start | bytes 1572868
  8.4 0.7 copy-start.4
  9.2 0.7 copy-start.5
  9.9 0.7 copy-start.6
  10.5 0.7 copy-start.7
  11.2 0.7 copy-start.8
  11.9 0.7 copy-start.9
  12.6 0.7 copy-start.10
  13.2 0.7 copy-start.11
  13.9 0.7 copy-start.12

commit v2 on v0

v2 whole, which is shorter than its diff:
```python
import functools

import jax
import jax.numpy as jnp
from jax import lax
from jax.experimental import pallas as pl
from jax.experimental.pallas import tpu as pltpu
from jax.sharding import PartitionSpec as P

GROUPS = 4
EPSILON = 1e-05
MESH = pl.DeviceIdType.MESH
F32 = jnp.float32
BF16 = jnp.bfloat16
LANES = 128
EMB_PIECES = 4


def silu(x):
    return x * (1.0 / (1.0 + jnp.exp(-x)))


def softplus(x):
    return jnp.maximum(x, 0.0) + jnp.log1p(jnp.exp(-jnp.abs(x)))


def iota(shape, axis):
    return lax.broadcasted_iota(jnp.int32, shape, axis)


def keep_rows(kids, counts):
    counted = counts[0]
    for i in range(1, kids - 1):
        counted = counted + counts[i]
    running = kids - counted
    marks = [running]
    for i in range(kids - 1):
        running = running + counts[i]
        marks.append(running)
    parent = []
    for k in range(kids):
        at = jnp.int32(0)
        for mark in marks:
            at = at + (mark <= k).astype(jnp.int32)
        parent.append(jnp.minimum(at, kids - 1))
    return parent


def apart(blocks, kids):
    whole = jnp.concatenate(blocks, axis=0)
    child = iota(whole.shape, 0) % kids
    return jnp.concatenate(
        [jnp.where(child == k, whole, 0.0) for k in range(kids)], axis=1
    ).astype(BF16)


def fused(
    np_,
    nh,
    counts_h,
    step_bias_h,
    decay_log_h,
    skip_gain_h,
    tok_h,
    kern_value_h,
    bias_value_h,
    kern_wread,
    bias_wread,
    norm_gain_h,
    ssm,
    conv_value,
    conv_wread,
    emb,
    w_gate,
    w_value,
    w_wread,
    w_step,
    w_output,
    parts_o,
    below_o,
    kept_o,
    added_o,
    writes_o,
    conv_o,
    counts,
    step_bias,
    decay_log,
    skip_gain,
    tok,
    ids_s,
    kern_value,
    bias_value,
    bw_v,
    norm_gain,
    emb_v,
    wg_v,
    wv_v,
    ww_v,
    ws_v,
    wo_v,
    win,
    cwin,
    wwin,
    kw_v,
    sbf,
    hist,
    whist,
    tok_part,
    tok_recv,
    tok_all,
    term_w,
    term_v,
    term_g,
    sib_w,
    sib_v,
    sib_g,
    out_w,
    out_v,
    out_g,
    in_w,
    in_v,
    in_g,
    quarter,
    nrm_all,
    part,
    kept_v,
    added_v,
    writes_v,
    conv_v,
    tok_sem,
    emb_sem,
    loc_sem,
    shift_send,
    shift_recv,
    rs_send,
    rs_recv,
    ag_send,
    ag_recv,
    sib_send,
    sib_recv,
    z_send,
    z_recv,
    mate_send,
    mate_recv,
    nrm_send,
    nrm_recv,
    fwd_send,
    fwd_recv,
    out_send,
    out_recv,
    own_sem,
    res_sem,
):
    p = lax.axis_index("particle")
    h = lax.axis_index("head")
    zs = np_ // 2
    z = p // 2
    c = p % 2
    sibling = z * 2 + 1 - c
    kids = counts.shape[0]
    steps = tok.shape[0]
    own = kids * steps
    rows = np_ * own
    width = wv_v.shape[1]
    state = ssm.shape[3]
    heads = ssm.shape[1]
    headdim = ssm.shape[2]
    vocab = emb.shape[0]
    span = nh // GROUPS
    group, mate = h // span, h % span
    share = 2 * state // span
    half = rows // 2
    owned = half // nh
    reach = zs // 2
    order = [reach]
    for d in range(reach - 1, 0, -1):
        order += [d, -d]
    order.append(0)

    def chip(d):
        return lax.rem(z + d + zs, zs)

    barrier = pltpu.get_barrier_semaphore()

    def greet_head(j, _):
        pl.semaphore_signal(
            barrier, inc=1, device_id={"head": lax.rem(h + j, nh)}, device_id_type=MESH
        )
        return 0

    def greet_particle(j, _):
        pl.semaphore_signal(
            barrier, inc=1, device_id={"particle": lax.rem(p + j, np_)}, device_id_type=MESH
        )
        return 0

    lax.fori_loop(1, nh, greet_head, 0)
    lax.fori_loop(1, np_, greet_particle, 0)

    tok_copy = pltpu.make_async_copy(tok_h, tok, tok_sem)
    tok_copy.start()
    piece = vocab // EMB_PIECES
    emb_copies = [
        pltpu.make_async_copy(
            emb.at[pl.ds(i * piece, piece)], emb_v.at[pl.ds(i * piece, piece)], emb_sem.at[i]
        )
        for i in range(EMB_PIECES)
    ]
    for copy in emb_copies:
        copy.start()
    at_write = pl.ds(pl.multiple_of(group * state, state), state)
    at_read = pl.ds(pl.multiple_of((GROUPS + group) * state, state), state)
    side = mate // (span // 2)
    at_share = pl.ds(pl.multiple_of((side * GROUPS + group) * state, state), state)
    lo, hi = pl.ds(0, state), pl.ds(state, state)
    pairs = [
        (ssm.at[pl.ds(0, kids - 1)], win.at[pl.ds(1, kids - 1)]),
        (conv_value, cwin.at[1]),
        (conv_wread.at[:, :, at_write], wwin.at[1, :, :, lo]),
        (conv_wread.at[:, :, at_read], wwin.at[1, :, :, hi]),
        (counts_h, counts),
        (w_wread.at[:, at_share], ww_v),
        (w_step, ws_v),
        (w_value, wv_v),
        (w_gate, wg_v),
        (kern_wread.at[:, at_write], kw_v.at[:, lo]),
        (kern_wread.at[:, at_read], kw_v.at[:, hi]),
        (w_output, wo_v),
        (step_bias_h, step_bias),
        (decay_log_h, decay_log),
        (skip_gain_h, skip_gain),
        (kern_value_h, kern_value),
        (bias_value_h, bias_value),
        (norm_gain_h, norm_gain),
        (bias_wread.at[:, at_write], bw_v.at[:, lo]),
        (bias_wread.at[:, at_read], bw_v.at[:, hi]),
    ]
    loads = [pltpu.make_async_copy(s, d, loc_sem.at[i]) for i, (s, d) in enumerate(pairs)]
    for copy in loads:
        copy.start()

    tok_copy.wait()
    ids_t = jnp.concatenate([tok[...], jnp.zeros((8 - steps, np_ * kids), jnp.int32)], axis=0).T
    ids_s[...] = ids_t - h * vocab

    def lookup(m):
        column = []
        for d in order[m * reach : (m + 1) * reach]:
            pair = ids_s[pl.ds(pl.multiple_of(chip(d) * 2 * kids, 2 * kids), 2 * kids), :]
            for core in range(2):
                for t in range(steps):
                    column.append(pair[core * kids : (core + 1) * kids, t : t + 1])
        ids = jnp.concatenate(column, axis=0)
        total = None
        for i in range(EMB_PIECES):
            if m == 0:
                emb_copies[i].wait()
            hot = jnp.where(ids - i * piece == iota((half, piece), 1), 1.0, 0.0).astype(BF16)
            term = jnp.dot(hot, emb_v[pl.ds(i * piece, piece)], preferred_element_type=F32)
            total = term if total is None else total + term
        tok_part[m] = total.astype(BF16).reshape(nh, owned, -1)

    def rs_copy(m, j):
        dest = lax.rem(h + j, nh)
        return pltpu.make_async_remote_copy(
            src_ref=tok_part.at[m, dest],
            dst_ref=tok_recv.at[m, j - 1],
            send_sem=rs_send.at[m, j - 1],
            recv_sem=rs_recv.at[m, j - 1],
            device_id={"head": dest},
            device_id_type=MESH,
        )

    def ag_copy(m, j):
        return pltpu.make_async_remote_copy(
            src_ref=tok_all.at[m, h],
            dst_ref=tok_all.at[m, h],
            send_sem=ag_send.at[m, j - 1],
            recv_sem=ag_recv.at[m, j - 1],
            device_id={"head": lax.rem(h + j, nh)},
            device_id_type=MESH,
        )

    def ag_back(m, j):
        source = lax.rem(h + nh - j, nh)
        return pltpu.make_async_remote_copy(
            src_ref=tok_all.at[m, h],
            dst_ref=tok_all.at[m, source],
            send_sem=ag_send.at[m, j - 1],
            recv_sem=ag_recv.at[m, j - 1],
            device_id={"head": source},
            device_id_type=MESH,
        )

    def each(do):
        def step(j, _):
            do(j)
            return 0

        lax.fori_loop(1, nh, step, 0)

    lookup(0)
    pl.semaphore_wait(barrier, nh - 1 + np_ - 1)
    each(lambda j: rs_copy(0, j).start())

    above = lax.rem(p + 1, np_)
    shift_pairs = [
        (ssm.at[kids - 1], win.at[0]),
        (conv_value, cwin.at[0]),
        (conv_wread.at[:, :, at_write], wwin.at[0, :, :, lo]),
        (conv_wread.at[:, :, at_read], wwin.at[0, :, :, hi]),
    ]
    shifts = [
        pltpu.make_async_remote_copy(
            src_ref=s,
            dst_ref=d,
            send_sem=shift_send.at[i],
            recv_sem=shift_recv.at[i],
            device_id={"particle": above},
            device_id_type=MESH,
        )
        for i, (s, d) in enumerate(shift_pairs)
    ]
    for copy in shifts:
        copy.start()
    lookup(1)
    each(lambda j: rs_copy(1, j).start())

    for m in range(2):
        each(lambda j, m=m: rs_copy(m, j).wait_recv())
        shared = tok_part[m, h]
        for s in range(nh - 1):
            shared = shared + tok_recv[m, s]
        tok_all[m, h] = shared
        each(lambda j, m=m: ag_copy(m, j).start())

    for copy in loads[:5]:
        copy.wait()
    parent = keep_rows(kids, counts)
    for copy in shifts:
        copy.wait_recv()
    below = pltpu.make_async_copy(win.at[0], below_o, res_sem.at[0])
    below.start()
    for k in range(kids):
        sbf[:, pl.ds(k * state, state)] = win[parent[k]].reshape(width, state).astype(BF16)
        here = jnp.minimum(parent[k], 1)
        row = pl.ds(jnp.where(parent[k] == 0, kids - 1, parent[k] - 1), 1)
        for tap in range(3):
            hist[tap, pl.ds(k, 1), :] = cwin[here, tap, row, :]
            whist[tap, pl.ds(k, 1), :] = wwin[here, tap, row, :]
    for copy in loads[5:]:
        copy.wait()

    kinds = [
        (term_w, sib_w, out_w, in_w),
        (term_v, sib_v, out_v, in_v),
        (term_g, sib_g, out_g, in_g),
    ]

    def sib_copy(kind, m):
        source, target = kinds[kind][:2]
        return pltpu.make_async_remote_copy(
            src_ref=source.at[1 - c, pl.ds(m * reach, reach)],
            dst_ref=target.at[pl.ds(m * reach, reach)],
            send_sem=sib_send.at[kind, m],
            recv_sem=sib_recv.at[kind, m],
            device_id={"particle": sibling},
            device_id_type=MESH,
        )

    def z_copy(kind, i):
        _, _, out, back = kinds[kind]
        return pltpu.make_async_remote_copy(
            src_ref=out.at[i],
            dst_ref=back.at[i],
            send_sem=z_send.at[kind, i],
            recv_sem=z_recv.at[kind, i],
            device_id={"particle": lax.rem(p + 2 * order[i] + np_, np_)},
            device_id_type=MESH,
        )

    def place(kind, m, terms):
        source = kinds[kind][0]
        for b in range(2 * reach):
            source[b % 2, m * reach + b // 2] = terms[b * own : (b + 1) * own].astype(BF16)
        sib_copy(kind, m).start()

    def chip_sum(kind, i):
        return kinds[kind][0][c, i].astype(F32) + kinds[kind][1][i].astype(F32)

    def send_sums(kind, m):
        sib_copy(kind, m).wait_recv()
        for i in range(m * reach, min((m + 1) * reach, zs - 1)):
            kinds[kind][2][i] = chip_sum(kind, i).astype(BF16)
            z_copy(kind, i).start()

    def arrive(kind):
        total = chip_sum(kind, zs - 1)
        for i in range(zs - 1):
            z_copy(kind, i).wait_recv()
            total = total + kinds[kind][3][i].astype(F32)
        return total.astype(BF16)

    for m in range(2):
        each(lambda j, m=m: ag_back(m, j).wait_recv())
        tokens = tok_all[m].reshape(half, -1)
        matrices = jnp.dot(tokens, ww_v[...], preferred_element_type=F32)
        rate = lax.dot_general(
            tokens, ws_v[...], (((1,), (1,)), ((), ())), preferred_element_type=F32
        )
        pads = [jnp.zeros((half, n), F32) for n in (share, LANES - share - heads)]
        rate = jnp.concatenate([pads[0], rate, pads[1]], axis=1)
        turned = jnp.concatenate([matrices[:, share:], matrices[:, :share]], axis=1)
        matrices = jnp.where(mate % (span // 2) == 0, matrices, turned)
        place(0, m, jnp.where(iota((half, LANES), 1) < share, matrices, rate))
        place(1, m, jnp.dot(tokens, wv_v[...], preferred_element_type=F32))
        place(2, m, jnp.dot(tokens, wg_v[...], preferred_element_type=F32))
        send_sums(0, m)
        send_sums(1, m)
    for m in range(2):
        send_sums(2, m)

    narrow = arrive(0)
    quarter[mate] = narrow

    def mate_copy(j):
        return pltpu.make_async_remote_copy(
            src_ref=quarter.at[mate],
            dst_ref=quarter.at[mate],
            send_sem=mate_send.at[j - 1],
            recv_sem=mate_recv.at[j - 1],
            device_id={"head": group * span + lax.rem(mate + j, span)},
            device_id_type=MESH,
        )

    def mate_back(j):
        source = lax.rem(mate + span - j, span)
        return pltpu.make_async_remote_copy(
            src_ref=quarter.at[mate],
            dst_ref=quarter.at[source],
            send_sem=mate_send.at[j - 1],
            recv_sem=mate_recv.at[j - 1],
            device_id={"head": group * span + source},
            device_id_type=MESH,
        )

    for j in range(1, span):
        mate_copy(j).start()

    def at_step(a, t):
        return a[t * kids : (t + 1) * kids]

    spread = (
        iota((LANES, width), 1) // headdim + share == iota((LANES, width), 0)
    ).astype(F32)
    rates = jnp.dot(narrow, spread.astype(BF16), preferred_element_type=F32)
    lane_head = iota((1, width), 1) // headdim

    def per_head(ref):
        out = jnp.zeros((1, width), F32)
        for i in range(heads):
            out = jnp.where(lane_head == i, ref[i], out)
        return out

    step_size = softplus(rates + per_head(step_bias))
    decay = jnp.exp(-step_size * jnp.exp(per_head(decay_log)))
    skip = per_head(skip_gain)

    def convolve(past, current, kern, bias):
        seq = [past[i] for i in range(3)] + [at_step(current, t) for t in range(steps)]
        out = []
        for t in range(steps):
            a = seq[t] * kern[0:1]
            for i in range(1, 4):
                a = a + seq[t + i] * kern[i : i + 1]
            out.append(silu(a + bias))
        return out

    for j in range(1, span):
        mate_back(j).wait_recv()
    wread = jnp.concatenate([quarter[i].astype(F32)[:, :share] for i in range(span)], axis=1)
    conv_w = convolve(whist, wread, kw_v[...], bw_v[...])
    writes = [a[:, :state] for a in conv_w]
    reads = [a[:, state:] for a in conv_w]
    first = lax.dot_general(
        apart(reads, kids), sbf[...], (((1,), (1,)), ((), ())), preferred_element_type=F32
    )
    value = arrive(1).astype(F32)
    conv = convolve(hist, value, kern_value[...], bias_value[...])

    kept = None
    added = []
    readings = []
    for t in range(steps):
        now = at_step(decay, t)
        kept = now if kept is None else kept * now
        added = [a * now for a in added] + [at_step(step_size, t) * conv[t]]
        reading = kept * at_step(first, t) + skip * conv[t]
        for u in range(t + 1):
            match = jnp.sum(writes[u] * reads[t], axis=1, keepdims=True)
            reading = reading + added[u] * match
        readings.append(reading)
    kept_v[...] = kept
    added_v[...] = jnp.concatenate(added, axis=0)
    writes_v[...] = jnp.concatenate(writes, axis=0)
    for i in range(3):
        conv_v[i] = at_step(value, steps - 3 + i)
    results = [
        pltpu.make_async_copy(s, d, res_sem.at[i + 1])
        for i, (s, d) in enumerate(
            [(kept_v, kept_o), (added_v, added_o), (writes_v, writes_o), (conv_v, conv_o)]
        )
    ]
    for copy in results:
        copy.start()
    gated = jnp.concatenate(readings, axis=0) * silu(arrive(2).astype(F32))

    squares = jnp.sum(gated * gated, axis=1, keepdims=True)
    upper = squares.astype(BF16).astype(F32)
    lane = iota((own, LANES), 1)
    squares = jnp.where(lane % 2 == 0, upper, squares - upper).astype(BF16)
    scaled = jnp.concatenate([(gated * norm_gain[...]).astype(BF16), squares], axis=1)
    at_row, from_row = iota((own, own), 0), iota((own, own), 1)
    turn = (from_row == (at_row % steps) * kids + at_row // steps).astype(F32).astype(BF16)
    scaled = jnp.dot(turn, scaled, preferred_element_type=F32)
    bands, cuts = own // 16, width // LANES
    marks = scaled[:16, width:]
    for r in range(bands):
        band = scaled[r * 16 : (r + 1) * 16]
        for i in range(cuts):
            nrm_all[p, r * cuts + i] = band[:, i * LANES : (i + 1) * LANES].astype(BF16)
        if r > 0:
            marks = jnp.where(iota(marks.shape, 1) < 2 * r, marks, band[:, width:])
    nrm_all[p, bands * cuts] = marks.astype(BF16)

    def nrm_copy(at, target, send, recv):
        return pltpu.make_async_remote_copy(
            src_ref=nrm_all.at[at],
            dst_ref=nrm_all.at[at],
            send_sem=send,
            recv_sem=recv,
            device_id={"particle": target},
            device_id_type=MESH,
        )

    def direct(i):
        target = lax.rem(p + 2 * order[i] + np_, np_)
        return nrm_copy(p, target, nrm_send.at[i], nrm_recv.at[i])

    def forward(i):
        at = lax.rem(p - 2 * order[i] + np_, np_)
        return nrm_copy(at, sibling, fwd_send.at[i], fwd_recv.at[i])

    for i in range(zs - 1):
        direct(i).start()
    forward(zs - 1).start()

    def dest_of(i, core):
        return lax.rem(z - order[i] + zs, zs) * 2 + core

    def out_copy(i, core):
        return pltpu.make_async_remote_copy(
            src_ref=part.at[i, core],
            dst_ref=parts_o.at[h],
            send_sem=out_send.at[i, core],
            recv_sem=out_recv.at[h],
            device_id={"head": dest_of(i, core)},
            device_id_type=MESH,
        )

    def own_copy(i, core):
        return pltpu.make_async_copy(part.at[i, core], parts_o.at[h], own_sem)

    def send_parts(places):
        block = []
        for i in places:
            for core in range(2):
                tiles = nrm_all[dest_of(i, core)]
                for r in range(bands):
                    block.append(
                        jnp.concatenate([tiles[r * cuts + n] for n in range(cuts)], axis=1)
                    )
        product = jnp.dot(
            jnp.concatenate(block, axis=0), wo_v[...], preferred_element_type=F32
        ).astype(BF16)
        for n, i in enumerate(places):
            for core in range(2):
                for r in range(bands):
                    start = (2 * n + core) * own + r * 16
                    for e in range(cuts):
                        part[i, core, r * cuts + e] = product[
                            start : start + 16, e * LANES : (e + 1) * LANES
                        ]
                part[i, core, bands * cuts] = nrm_all[dest_of(i, core), bands * cuts]
        for i in places:
            for core in range(2):
                dest = dest_of(i, core)

                @pl.when(dest != h)
                def _(i=i, core=core):
                    out_copy(i, core).start()

                @pl.when(dest == h)
                def _(i=i, core=core):
                    own_copy(i, core).start()

    def take(i):
        at = lax.rem(p - 2 * order[i] + np_, np_)
        if order[i] != 0:
            nrm_copy(at, sibling, nrm_send.at[i], nrm_recv.at[i]).wait_recv()
            forward(i).start()

    def take_forward(i):
        at = lax.rem(sibling - 2 * order[i] + np_, np_)
        nrm_copy(at, sibling, fwd_send.at[i], fwd_recv.at[i]).wait_recv()

    near = list(range(zs))[::-1]
    batches = [near[: max(1, zs // 2 - 1)], near[max(1, zs // 2 - 1) :]]
    for batch in batches:
        for i in batch:
            take(i)
        for i in batch:
            take_forward(i)
        send_parts(batch)

    for m in range(2):
        each(lambda j, m=m: rs_copy(m, j).wait_send())
        each(lambda j, m=m: ag_copy(m, j).wait_send())
    for copy in shifts:
        copy.wait_send()
    for kind in range(3):
        for m in range(2):
            sib_copy(kind, m).wait_send()
        for i in range(zs - 1):
            z_copy(kind, i).wait_send()
    for j in range(1, span):
        mate_copy(j).wait_send()
    for i in range(zs - 1):
        direct(i).wait_send()
    for i in range(zs):
        forward(i).wait_send()
    below.wait()
    for copy in results:
        copy.wait()
    for i in range(zs):
        for core in range(2):
            dest = dest_of(i, core)

            @pl.when(dest != h)
            def _(i=i, core=core):
                out_copy(i, core).wait_send()

    own_copy(0, 0).wait()

    def out_wait(s, _):
        @pl.when(s != h)
        def _():
            pltpu.make_async_remote_copy(
                src_ref=part.at[0, 0],
                dst_ref=parts_o.at[s],
                send_sem=out_send.at[0, 0],
                recv_sem=out_recv.at[s],
                device_id={"head": s},
                device_id_type=MESH,
            ).wait_recv()

        return 0

    lax.fori_loop(0, nh, out_wait, 0)


def finish(
    nh,
    parts_h,
    below_h,
    kept_h,
    added_h,
    writes_h,
    conv_h,
    counts_h,
    ssm,
    mixed,
    final_state,
    final_conv,
    parts,
    kept,
    added,
    writes,
    counts,
    win,
    fin,
    load_sem,
    win_sem,
    out_sem,
):
    kids, heads, headdim, state = final_state.shape
    own = added.shape[0]
    steps = own // kids
    width = heads * headdim
    span = nh // GROUPS
    pairs = [
        (counts_h, counts),
        (kept_h, kept),
        (added_h, added),
        (writes_h, writes),
        (below_h, win.at[0]),
        (ssm.at[pl.ds(0, kids - 1)], win.at[pl.ds(1, kids - 1)]),
        (parts_h, parts),
        (conv_h, final_conv),
    ]
    loads = [pltpu.make_async_copy(s, d, load_sem.at[i]) for i, (s, d) in enumerate(pairs)]
    for copy in loads:
        copy.start()
    for copy in loads[:4]:
        copy.wait()
    parent = keep_rows(kids, counts)
    terms = lax.dot_general(
        added[...].astype(BF16),
        apart([writes[...]], kids),
        (((0,), (0,)), ((), ())),
        preferred_element_type=F32,
    )
    for copy in loads[4:6]:
        copy.wait()
    for k in range(kids):
        for i in range(heads):
            factor = jnp.broadcast_to(
                kept[k : k + 1, i * headdim : i * headdim + 1], (headdim, state)
            )
            fin[k, i] = (
                win[parent[k], i] * factor
                + terms[i * headdim : (i + 1) * headdim, k * state : (k + 1) * state]
            )
        pltpu.make_async_copy(fin.at[k], final_state.at[k], out_sem.at[k]).start()
    loads[6].wait()
    bands, cuts = own // 16, mixed.shape[2] // LANES
    for r in range(bands):
        answer = [jnp.zeros((16, LANES), F32) for _ in range(cuts)]
        for g in range(GROUPS):
            square = jnp.zeros((16, 1), F32)
            total = [jnp.zeros((16, LANES), F32) for _ in range(cuts)]
            for s in range(g * span, (g + 1) * span):
                mark = parts[s, bands * cuts].astype(F32)[:, 2 * r : 2 * r + 2]
                square = square + mark[:, 0:1] + mark[:, 1:2]
                for i in range(cuts):
                    total[i] = total[i] + parts[s, r * cuts + i].astype(F32)
            scale = lax.rsqrt(square / (width * span) + EPSILON)
            answer = [a + b * scale for a, b in zip(answer, total)]
        answer = jnp.concatenate(answer, axis=1)
        each = 16 // steps
        for k in range(each):
            mixed[r * each + k] = answer[k * steps : (k + 1) * steps].astype(BF16)
    loads[7].wait()
    for k in range(kids):
        pltpu.make_async_copy(fin.at[k], final_state.at[k], out_sem.at[k]).wait()


def on_device(
    np_,
    nh,
    counts,
    ssm_state,
    conv_value,
    conv_wread,
    token_ids,
    embedding,
    w_gate,
    w_value,
    w_wread,
    w_step,
    kern_value,
    bias_value,
    kern_wread,
    bias_wread,
    step_bias,
    decay_log,
    skip_gain,
    norm_gain,
    w_output,
):
    kids, heads, headdim, state = ssm_state.shape
    steps = token_ids.shape[1]
    own = kids * steps
    rows = np_ * own
    owned = rows // 2 // nh
    depth, width = w_value.shape
    cols = w_output.shape[1]
    zs = np_ // 2
    span = nh // GROUPS
    taps = kern_value.shape[0]
    tiles = own // 16 * (width // LANES) + 1
    dma = pltpu.SemaphoreType.DMA
    smem = pltpu.SMEM
    vmem = pltpu.VMEM
    scratch = [
        smem((kids,), jnp.int32),
        smem((heads,), F32),
        smem((heads,), F32),
        smem((heads,), F32),
        vmem((steps, np_ * kids), jnp.int32),
        vmem((np_ * kids, 8), jnp.int32),
        vmem((taps, width), F32),
        vmem((1, width), F32),
        vmem((1, 2 * state), F32),
        vmem((1, width), F32),
        vmem(embedding.shape, BF16),
        vmem((depth, width), BF16),
        vmem((depth, width), BF16),
        vmem((depth, state), BF16),
        vmem((heads, depth), BF16),
        vmem((width, cols), BF16),
        vmem((kids, heads, headdim, state), F32),
        vmem((2, 3, kids, width), F32),
        vmem((2, 3, kids, 2 * state), F32),
        vmem((taps, 2 * state), F32),
        vmem((width, kids * state), BF16),
        vmem((3, kids, width), F32),
        vmem((3, kids, 2 * state), F32),
        vmem((2, nh, owned, depth), BF16),
        vmem((2, nh - 1, owned, depth), BF16),
        vmem((2, nh, owned, depth), BF16),
        vmem((2, zs, own, LANES), BF16),
        vmem((2, zs, own, width), BF16),
        vmem((2, zs, own, width), BF16),
        vmem((zs, own, LANES), BF16),
        vmem((zs, own, width), BF16),
        vmem((zs, own, width), BF16),
        vmem((zs - 1, own, LANES), BF16),
        vmem((zs - 1, own, width), BF16),
        vmem((zs - 1, own, width), BF16),
        vmem((zs - 1, own, LANES), BF16),
        vmem((zs - 1, own, width), BF16),
        vmem((zs - 1, own, width), BF16),
        vmem((span, own, LANES), BF16),
        vmem((np_, tiles, 16, LANES), BF16),
        vmem((zs, 2, tiles, 16, LANES), BF16),
        vmem((kids, width), F32),
        vmem((own, width), F32),
        vmem((own, state), F32),
        vmem((3, kids, width), F32),
        dma,
        dma((EMB_PIECES,)),
        dma((20,)),
        dma((4,)),
        dma((4,)),
        dma((2, nh - 1)),
        dma((2, nh - 1)),
        dma((2, nh - 1)),
        dma((2, nh - 1)),
        dma((3, 2)),
        dma((3, 2)),
        dma((3, zs - 1)),
        dma((3, zs - 1)),
        dma((span - 1,)),
        dma((span - 1,)),
        dma((zs - 1,)),
        dma((zs - 1,)),
        dma((zs,)),
        dma((zs,)),
        dma((zs, 2)),
        dma((nh,)),
        dma,
        dma((5,)),
    ]
    hbm = pl.BlockSpec(memory_space=pltpu.HBM)
    limit = 60 * 1024 * 1024
    shape = jax.ShapeDtypeStruct
    parts, below, kept, added, writes, conv = pl.pallas_call(
        functools.partial(fused, np_, nh),
        out_shape=(
            shape((nh, tiles, 16, LANES), BF16),
            shape((heads, headdim, state), F32),
            shape((kids, width), F32),
            shape((own, width), F32),
            shape((own, state), F32),
            shape((3, kids, width), F32),
        ),
        in_specs=[hbm] * 19,
        out_specs=(hbm,) * 6,
        scratch_shapes=scratch,
        compiler_params=pltpu.CompilerParams(
            collective_id=0, has_side_effects=True, vmem_limit_bytes=limit
        ),
    )(
        counts,
        step_bias,
        decay_log,
        skip_gain,
        token_ids.T,
        kern_value,
        bias_value.reshape(1, -1),
        kern_wread,
        bias_wread.reshape(1, -1),
        norm_gain.reshape(1, -1),
        ssm_state,
        conv_value.transpose(1, 0, 2),
        conv_wread.transpose(1, 0, 2),
        embedding,
        w_gate,
        w_value,
        w_wread,
        w_step.T,
        w_output,
    )
    mixed, final_state, final_conv = pl.pallas_call(
        functools.partial(finish, nh),
        out_shape=(
            shape((kids, steps, cols), BF16),
            shape(ssm_state.shape, F32),
            shape((3, kids, width), F32),
        ),
        in_specs=[hbm] * 8,
        out_specs=(pl.BlockSpec(memory_space=pltpu.VMEM), hbm, hbm),
        scratch_shapes=[
            vmem((nh, tiles, 16, LANES), BF16),
            vmem((kids, width), F32),
            vmem((own, width), F32),
            vmem((own, state), F32),
            smem((kids,), jnp.int32),
            vmem((kids, heads, headdim, state), F32),
            vmem((kids, heads, headdim, state), F32),
            dma((8,)),
            dma,
            dma((kids,)),
        ],
        compiler_params=pltpu.CompilerParams(vmem_limit_bytes=limit),
    )(parts, below, kept, added, writes, conv, counts, ssm_state)
    return mixed, final_state, final_conv.transpose(1, 0, 2)


def solution(mesh):
    return jax.shard_map(
        functools.partial(on_device, mesh.shape["particle"], mesh.shape["head"]),
        mesh=mesh,
        in_specs=(
            P("particle"),
            P("particle", "head", None, None),
            P("particle", None, "head"),
            P("particle", None, None),
            P(),
            P("head", "particle"),
            P("particle", "head"),
            P("particle", "head"),
            P("particle", None),
            P("particle", "head"),
            P(None, "head"),
            P("head"),
            P(),
            P(),
            P("head"),
            P("head"),
            P("head"),
            P("head"),
            P("head", "particle"),
        ),
        out_specs=(
            P("head", None, "particle"),
            P("particle", "head", None, None),
            P("particle", None, "head"),
        ),
        check_vma=False,
    )
```

time: 326 us -> 71.6 us (0.22)
  waiting for transfers between devices: 189 us -> 0 us
  Pallas kernels: 0 us -> 69.6 us
  local copies, waits for them, and re-layouts: 37.3 us -> 0 us
  blocking collectives: 36.7 us -> 0 us
  other arithmetic: 24.5 us -> 0 us
  between operations: 15.5 us -> 0.65 us
  matrix products: 9.74 us -> 0 us
  starting transfers between devices: 8.32 us -> 0 us
    reduce_scatter x2 -> x0, waiting for transfers between devices: 127 us -> none  [the longest x1 72.6 us: on_device(): lax.psum_scatter(jnp.dot(every_row, w_output, preferred_element_type=jnp....]
    pallas_call x0 -> x2, Pallas kernels: none -> 69.6 us  [the longest x1 65.8 us: on_device(): pl.pallas_call(functools.partial(fused, np_, nh), out_shape=(shape((nh, t...]
    psum x1 -> x0, waiting for transfers between devices: 59.8 us -> none  [on_device(): tokens = lax.psum(partial_rows.astype(jnp.bfloat16), 'head')]
    all_gather x1 -> x0, blocking collectives: 21.7 us -> none  [on_device(): every_row = lax.all_gather(normed, 'particle', axis=0, tiled=True)]
    unnamed x1 -> x0, blocking collectives: 15 us -> none
    reduce_sum x7 -> x0, other arithmetic: 9.91 us -> none  [the longest x1 7.47 us: on_device(): jnp.sum(states * reads[:, :, None, :], axis=3)]
    dot_general x5 -> x0, matrix products: 9.74 us -> none  [the longest x4 7.47 us: projector(): jnp.dot(tokens, weight, preferred_element_type=jnp.float32)]
    gather x2 -> x0, local copies, waits for them, and re-layouts: 9.36 us -> none  [the longest x1 4.72 us: on_device(): looked = jnp.take(embedding, jnp.clip(shifted, 0, vocab_rows - 1), axis=0)]
  transfers between devices with their start and end apart: 6 -> 0, of which waited for: 5 -> 0; matrix products, arithmetic and copies ran while one was open for 11% -> 0% of each run, Pallas kernels for 0% -> 0%
where the time goes in v2:
time: 71.6 us; the launch traced here: 70.3 us
  Pallas kernels  69.6 us (97%)
    pallas_call x1, Pallas kernels, on_device(): pl.pallas_call(functools.partial(fused, np_, nh), out_shape=(shape((nh, t...  65.8 us
    pallas_call x1, Pallas kernels, on_device(): pl.pallas_call(functools.partial(finish, nh), out_shape=(shape((kids, ste...  3.82 us

profile of v2, /device:TPU:5, one launch (start us, length us, event | category | flops | bytes accessed | tf_op | source)
XLA Modules:
  0.0 70.3 jit_solution(11881256109149202600)
XLA Ops:
  0.6 65.8 %shard_map.202 = (bf16[16,9,16,128]{3,2,1,0:T(8,128)(2,1)}, f32[8,64,128]{2,1,0:T(8,128)}, f32[8,512]{1,0:T(8,128)}, f32[32,512]{1,0:T(8,128)}, f32[32,128]{1,0:T(8,128)}, /*index=5*/f32[3,8,512]{2,1,0:T(8,128)}) custom-call(s32[8]{0:T(128)} %counts_h.3, f32[8]{0:T(128)} %step_bias_h.1, f32[8]{0:T(128)} %decay_log_h.1, f32[8]{0:T(128)} %skip_gain_h.1, ...), custom_call_target="tpu_custom_call" | custom-call | tf_op jit(solution)/shard_map/pallas_call | solution.py:868
  66.4 3.8 %shard_map.203 = (bf16[8,4,512]{2,1,0:T(4,128)(2,1)}, f32[8,8,64,128]{3,2,1,0:T(8,128)}, f32[3,8,512]{2,1,0:T(8,128)}) custom-call(bf16[16,9,16,128]{3,2,1,0:T(8,128)(2,1)} %get-tuple-element.12.parts_h, f32[8,64,128]{2,1,0:T(8,128)} %get-tuple-element.13.below_h, f32[8,512]{1,0:T(8,128)} %get-tuple-element.14.kept_h, f32[32,512]{1,0:T(8,128)} %get-tuple-element.15.added_h, ...), custom_call_target="tpu_custom_call" | custom-call | tf_op jit(solution)/shard_map/pallas_call | solution.py:905

commit v3 on v2

--- a/solution.py
+++ b/solution.py
@@ -77,10 +77,7 @@
     w_step,
     w_output,
     parts_o,
-    below_o,
-    kept_o,
-    added_o,
-    writes_o,
+    states_o,
     conv_o,
     counts,
     step_bias,
@@ -116,16 +113,16 @@
     sib_g,
     out_w,
     out_v,
-    out_g,
+    out_far,
+    out_near,
     in_w,
     in_v,
-    in_g,
+    in_far,
+    in_near,
     quarter,
     nrm_all,
     part,
-    kept_v,
-    added_v,
-    writes_v,
+    fin,
     conv_v,
     tok_sem,
     emb_sem,
@@ -140,6 +137,10 @@
     sib_recv,
     z_send,
     z_recv,
+    far_send,
+    far_recv,
+    near_send,
+    near_recv,
     mate_send,
     mate_recv,
     nrm_send,
@@ -339,8 +340,6 @@
     parent = keep_rows(kids, counts)
     for copy in shifts:
         copy.wait_recv()
-    below = pltpu.make_async_copy(win.at[0], below_o, res_sem.at[0])
-    below.start()
     for k in range(kids):
         sbf[:, pl.ds(k * state, state)] = win[parent[k]].reshape(width, state).astype(BF16)
         here = jnp.minimum(parent[k], 1)
@@ -354,7 +353,7 @@
     kinds = [
         (term_w, sib_w, out_w, in_w),
         (term_v, sib_v, out_v, in_v),
-        (term_g, sib_g, out_g, in_g),
+        (term_g, sib_g),
     ]
 
     def sib_copy(kind, m):
@@ -368,6 +367,9 @@
             device_id_type=MESH,
         )
 
+    def along(d):
+        return {"particle": lax.rem(p + 2 * d + np_, np_)}
+
     def z_copy(kind, i):
         _, _, out, back = kinds[kind]
         return pltpu.make_async_remote_copy(
@@ -375,22 +377,22 @@
             dst_ref=back.at[i],
             send_sem=z_send.at[kind, i],
             recv_sem=z_recv.at[kind, i],
-            device_id={"particle": lax.rem(p + 2 * order[i] + np_, np_)},
+            device_id=along(order[i]),
             device_id_type=MESH,
         )
 
     def place(kind, m, terms):
         source = kinds[kind][0]
         for b in range(2 * reach):
-            source[b % 2, m * reach + b // 2] = terms[b * own : (b + 1) * own].astype(BF16)
+            block = terms[b * own : (b + 1) * own].astype(BF16)
+            source[b % 2, m * reach + b // 2] = block.reshape(source.shape[2:])
         sib_copy(kind, m).start()
 
     def chip_sum(kind, i):
         return kinds[kind][0][c, i].astype(F32) + kinds[kind][1][i].astype(F32)
 
-    def send_sums(kind, m):
-        sib_copy(kind, m).wait_recv()
-        for i in range(m * reach, min((m + 1) * reach, zs - 1)):
+    def send_sums(kind, which):
+        for i in which:
             kinds[kind][2][i] = chip_sum(kind, i).astype(BF16)
             z_copy(kind, i).start()
 
@@ -401,6 +403,38 @@
             total = total + kinds[kind][3][i].astype(F32)
         return total.astype(BF16)
 
+    def gate_sum(d, q):
+        i = order.index(d)
+        return term_g[c, i, q].astype(F32) + sib_g[i, q].astype(F32)
+
+    def whole(q, way):
+        return (way == 1) == (q == 0)
+
+    def far_copy(q, way):
+        side = (1 - way) // 2
+        cut = pl.ds(0, 2) if whole(q, way) else pl.ds(1, 1)
+        return pltpu.make_async_remote_copy(
+            src_ref=out_far.at[q, side, cut],
+            dst_ref=in_far.at[q, side, cut],
+            send_sem=far_send.at[q, side],
+            recv_sem=far_recv.at[q, side],
+            device_id=along(2 * way),
+            device_id_type=MESH,
+        )
+
+    def near_copy(q, way, n):
+        side = (1 - way) // 2
+        return pltpu.make_async_remote_copy(
+            src_ref=out_near.at[q, side, n],
+            dst_ref=in_near.at[q, side, n],
+            send_sem=near_send.at[q, side, n],
+            recv_sem=near_recv.at[q, side, n],
+            device_id=along((2 - n) * way),
+            device_id_type=MESH,
+        )
+
+    legs = [(q, way) for q in range(2) for way in (1, -1)]
+
     for m in range(2):
         each(lambda j, m=m: ag_back(m, j).wait_recv())
         tokens = tok_all[m].reshape(half, -1)
@@ -413,12 +447,37 @@
         turned = jnp.concatenate([matrices[:, share:], matrices[:, :share]], axis=1)
         matrices = jnp.where(mate % (span // 2) == 0, matrices, turned)
         place(0, m, jnp.where(iota((half, LANES), 1) < share, matrices, rate))
+        place(2, m, jnp.dot(tokens, wg_v[...], preferred_element_type=F32))
         place(1, m, jnp.dot(tokens, wv_v[...], preferred_element_type=F32))
-        place(2, m, jnp.dot(tokens, wg_v[...], preferred_element_type=F32))
-        send_sums(0, m)
-        send_sums(1, m)
-    for m in range(2):
-        send_sums(2, m)
+        sib_copy(0, m).wait_recv()
+        send_sums(0, range(m * reach, min((m + 1) * reach, zs - 1)))
+        sib_copy(2, m).wait_recv()
+        if m == 0:
+            for q, way in legs:
+                side = (1 - way) // 2
+                if whole(q, way):
+                    out_far[q, side, 0] = gate_sum(reach, q).astype(BF16)
+                out_far[q, side, 1] = gate_sum(way * (reach - 1), q).astype(BF16)
+                far_copy(q, way).start()
+        sib_copy(1, m).wait_recv()
+        send_sums(1, range(1) if m == 0 else range(1, zs - 1))
+    for q, way in legs:
+        side = (1 - way) // 2
+        far_copy(q, way).wait_recv()
+        for n in range(2):
+            term = gate_sum(way * (2 - n), q)
+            if n == 1 or whole(q, way):
+                term = term + in_far[q, side, n].astype(F32)
+            out_near[q, side, n] = term.astype(BF16)
+            near_copy(q, way, n).start()
+
+    def arrive_gate(q):
+        total = gate_sum(0, q)
+        for side, way in enumerate((1, -1)):
+            for n in range(2):
+                near_copy(q, way, n).wait_recv()
+                total = total + in_near[q, side, n].astype(F32)
+        return total.astype(BF16)
 
     narrow = arrive(0)
     quarter[mate] = narrow
@@ -500,20 +559,8 @@
             match = jnp.sum(writes[u] * reads[t], axis=1, keepdims=True)
             reading = reading + added[u] * match
         readings.append(reading)
-    kept_v[...] = kept
-    added_v[...] = jnp.concatenate(added, axis=0)
-    writes_v[...] = jnp.concatenate(writes, axis=0)
-    for i in range(3):
-        conv_v[i] = at_step(value, steps - 3 + i)
-    results = [
-        pltpu.make_async_copy(s, d, res_sem.at[i + 1])
-        for i, (s, d) in enumerate(
-            [(kept_v, kept_o), (added_v, added_o), (writes_v, writes_o), (conv_v, conv_o)]
-        )
-    ]
-    for copy in results:
-        copy.start()
-    gated = jnp.concatenate(readings, axis=0) * silu(arrive(2).astype(F32))
+    gate = jnp.concatenate([arrive_gate(q) for q in range(2)], axis=0).astype(F32)
+    gated = jnp.concatenate(readings, axis=0) * silu(gate)
 
     squares = jnp.sum(gated * gated, axis=1, keepdims=True)
     upper = squares.astype(BF16).astype(F32)
@@ -551,9 +598,33 @@
         at = lax.rem(p - 2 * order[i] + np_, np_)
         return nrm_copy(at, sibling, fwd_send.at[i], fwd_recv.at[i])
 
-    for i in range(zs - 1):
+    for i in reversed(range(zs - 1)):
         direct(i).start()
     forward(zs - 1).start()
+
+    adds = lax.dot_general(
+        jnp.concatenate(added, axis=0).astype(BF16),
+        apart(writes, kids),
+        (((0,), (0,)), ((), ())),
+        preferred_element_type=F32,
+    )
+    for k in range(kids):
+        for i in range(heads):
+            factor = jnp.broadcast_to(
+                kept[k : k + 1, i * headdim : i * headdim + 1], (headdim, state)
+            )
+            fin[k, i] = (
+                win[parent[k], i] * factor
+                + adds[i * headdim : (i + 1) * headdim, k * state : (k + 1) * state]
+            )
+    for i in range(3):
+        conv_v[i] = at_step(value, steps - 3 + i)
+    results = [
+        pltpu.make_async_copy(s, d, res_sem.at[i])
+        for i, (s, d) in enumerate([(fin, states_o), (conv_v, conv_o)])
+    ]
+    for copy in results:
+        copy.start()
 
     def dest_of(i, core):
         return lax.rem(z - order[i] + zs, zs) * 2 + core
@@ -615,7 +686,7 @@
         nrm_copy(at, sibling, fwd_send.at[i], fwd_recv.at[i]).wait_recv()
 
     near = list(range(zs))[::-1]
-    batches = [near[: max(1, zs // 2 - 1)], near[max(1, zs // 2 - 1) :]]
+    batches = [near[:3], near[3:5], near[5:]]
     for batch in batches:
         for i in batch:
             take(i)
@@ -631,15 +702,19 @@
     for kind in range(3):
         for m in range(2):
             sib_copy(kind, m).wait_send()
+    for kind in range(2):
         for i in range(zs - 1):
             z_copy(kind, i).wait_send()
+    for q, way in legs:
+        far_copy(q, way).wait_send()
+        for n in range(2):
+            near_copy(q, way, n).wait_send()
     for j in range(1, span):
         mate_copy(j).wait_send()
     for i in range(zs - 1):
         direct(i).wait_send()
     for i in range(zs):
         forward(i).wait_send()
-    below.wait()
     for copy in results:
         copy.wait()
     for i in range(zs):
@@ -671,69 +746,36 @@
 
 def finish(
     nh,
+    steps,
     parts_h,
-    below_h,
-    kept_h,
-    added_h,
-    writes_h,
+    states_h,
     conv_h,
-    counts_h,
-    ssm,
     mixed,
     final_state,
     final_conv,
     parts,
-    kept,
-    added,
-    writes,
-    counts,
-    win,
-    fin,
-    load_sem,
-    win_sem,
-    out_sem,
+    states,
+    conv,
+    in_sems,
+    out_sems,
 ):
-    kids, heads, headdim, state = final_state.shape
-    own = added.shape[0]
-    steps = own // kids
+    kids, heads, headdim, _ = states_h.shape
     width = heads * headdim
     span = nh // GROUPS
-    pairs = [
-        (counts_h, counts),
-        (kept_h, kept),
-        (added_h, added),
-        (writes_h, writes),
-        (below_h, win.at[0]),
-        (ssm.at[pl.ds(0, kids - 1)], win.at[pl.ds(1, kids - 1)]),
-        (parts_h, parts),
-        (conv_h, final_conv),
-    ]
-    loads = [pltpu.make_async_copy(s, d, load_sem.at[i]) for i, (s, d) in enumerate(pairs)]
-    for copy in loads:
+    load = pltpu.make_async_copy(parts_h, parts, in_sems.at[kids + 1])
+    pairs = [(states_h.at[k], states.at[k], final_state.at[k]) for k in range(kids)]
+    pairs.append((conv_h, conv, final_conv))
+    pulls = [pltpu.make_async_copy(a, b, in_sems.at[i]) for i, (a, b, _) in enumerate(pairs)]
+    pushes = [pltpu.make_async_copy(b, d, out_sems.at[i]) for i, (_, b, d) in enumerate(pairs)]
+    for copy in pulls:
         copy.start()
-    for copy in loads[:4]:
-        copy.wait()
-    parent = keep_rows(kids, counts)
-    terms = lax.dot_general(
-        added[...].astype(BF16),
-        apart([writes[...]], kids),
-        (((0,), (0,)), ((), ())),
-        preferred_element_type=F32,
-    )
-    for copy in loads[4:6]:
-        copy.wait()
-    for k in range(kids):
-        for i in range(heads):
-            factor = jnp.broadcast_to(
-                kept[k : k + 1, i * headdim : i * headdim + 1], (headdim, state)
-            )
-            fin[k, i] = (
-                win[parent[k], i] * factor
-                + terms[i * headdim : (i + 1) * headdim, k * state : (k + 1) * state]
-            )
-        pltpu.make_async_copy(fin.at[k], final_state.at[k], out_sem.at[k]).start()
-    loads[6].wait()
-    bands, cuts = own // 16, mixed.shape[2] // LANES
+    load.start()
+    for pull, push in zip(pulls, pushes):
+        pull.wait()
+        push.start()
+    load.wait()
+    cuts = mixed.shape[2] // LANES
+    bands = (parts.shape[1] - 1) // cuts
     for r in range(bands):
         answer = [jnp.zeros((16, LANES), F32) for _ in range(cuts)]
         for g in range(GROUPS):
@@ -750,9 +792,8 @@
         each = 16 // steps
         for k in range(each):
             mixed[r * each + k] = answer[k * steps : (k + 1) * steps].astype(BF16)
-    loads[7].wait()
-    for k in range(kids):
-        pltpu.make_async_copy(fin.at[k], final_state.at[k], out_sem.at[k]).wait()
+    for copy in pushes:
+        copy.wait()
 
 
 def on_device(
@@ -821,22 +862,22 @@
         vmem((2, nh, owned, depth), BF16),
         vmem((2, zs, own, LANES), BF16),
         vmem((2, zs, own, width), BF16),
-        vmem((2, zs, own, width), BF16),
+        vmem((2, zs, 2, own // 2, width), BF16),
         vmem((zs, own, LANES), BF16),
         vmem((zs, own, width), BF16),
-        vmem((zs, own, width), BF16),
+        vmem((zs, 2, own // 2, width), BF16),
         vmem((zs - 1, own, LANES), BF16),
         vmem((zs - 1, own, width), BF16),
-        vmem((zs - 1, own, width), BF16),
+        vmem((2, 2, 2, own // 2, width), BF16),
+        vmem((2, 2, 2, own // 2, width), BF16),
         vmem((zs - 1, own, LANES), BF16),
         vmem((zs - 1, own, width), BF16),
-        vmem((zs - 1, own, width), BF16),
+        vmem((2, 2, 2, own // 2, width), BF16),
+        vmem((2, 2, 2, own // 2, width), BF16),
         vmem((span, own, LANES), BF16),
         vmem((np_, tiles, 16, LANES), BF16),
         vmem((zs, 2, tiles, 16, LANES), BF16),
-        vmem((kids, width), F32),
-        vmem((own, width), F32),
-        vmem((own, state), F32),
+        vmem(ssm_state.shape, F32),
         vmem((3, kids, width), F32),
         dma,
         dma((EMB_PIECES,)),
@@ -849,8 +890,12 @@
         dma((2, nh - 1)),
         dma((3, 2)),
         dma((3, 2)),
-        dma((3, zs - 1)),
-        dma((3, zs - 1)),
+        dma((2, zs - 1)),
+        dma((2, zs - 1)),
+        dma((2, 2)),
+        dma((2, 2)),
+        dma((2, 2, 2)),
+        dma((2, 2, 2)),
         dma((span - 1,)),
         dma((span - 1,)),
         dma((zs - 1,)),
@@ -860,23 +905,20 @@
         dma((zs, 2)),
         dma((nh,)),
         dma,
-        dma((5,)),
+        dma((2,)),
     ]
     hbm = pl.BlockSpec(memory_space=pltpu.HBM)
     limit = 60 * 1024 * 1024
     shape = jax.ShapeDtypeStruct
-    parts, below, kept, added, writes, conv = pl.pallas_call(
+    parts, states, conv = pl.pallas_call(
         functools.partial(fused, np_, nh),
         out_shape=(
             shape((nh, tiles, 16, LANES), BF16),
-            shape((heads, headdim, state), F32),
-            shape((kids, width), F32),
-            shape((own, width), F32),
-            shape((own, state), F32),
+            shape(ssm_state.shape, F32),
             shape((3, kids, width), F32),
         ),
         in_specs=[hbm] * 19,
-        out_specs=(hbm,) * 6,
+        out_specs=(hbm,) * 3,
         scratch_shapes=scratch,
         compiler_params=pltpu.CompilerParams(
             collective_id=0, has_side_effects=True, vmem_limit_bytes=limit
@@ -903,28 +945,23 @@
         w_output,
     )
     mixed, final_state, final_conv = pl.pallas_call(
-        functools.partial(finish, nh),
+        functools.partial(finish, nh, steps),
         out_shape=(
             shape((kids, steps, cols), BF16),
             shape(ssm_state.shape, F32),
             shape((3, kids, width), F32),
         ),
-        in_specs=[hbm] * 8,
+        in_specs=[hbm] * 3,
         out_specs=(pl.BlockSpec(memory_space=pltpu.VMEM), hbm, hbm),
         scratch_shapes=[
             vmem((nh, tiles, 16, LANES), BF16),
-            vmem((kids, width), F32),
-            vmem((own, width), F32),
-            vmem((own, state), F32),
-            smem((kids,), jnp.int32),
-            vmem((kids, heads, headdim, state), F32),
-            vmem((kids, heads, headdim, state), F32),
-            dma((8,)),
-            dma,
-            dma((kids,)),
+            vmem(ssm_state.shape, F32),
+            vmem((3, kids, width), F32),
+            dma((kids + 2,)),
+            dma((kids + 1,)),
         ],
         compiler_params=pltpu.CompilerParams(vmem_limit_bytes=limit),
-    )(parts, below, kept, added, writes, conv, counts, ssm_state)
+    )(parts, states, conv)
     return mixed, final_state, final_conv.transpose(1, 0, 2)
 
 

time: 71.6 us -> 67.3 us (0.940); the launches traced: 70.3 us -> 67.2 us
  Pallas kernels: 69.6 us -> 66.5 us
    pallas_call x1, Pallas kernels: 65.8 us -> 63.5 us  [on_device(): pl.pallas_call(functools.partial(fused, np_, nh), out_shape=(shape((nh, t...]
    pallas_call x1, Pallas kernels: 3.82 us -> 3.04 us  [on_device(): pl.pallas_call(functools.partial(finish, nh, steps), out_shape=(shape((ki...]
where the time goes in v3:
time: 67.3 us; the launch traced here: 67.2 us
  Pallas kernels  66.5 us (99%)
    pallas_call x1, Pallas kernels, on_device(): pl.pallas_call(functools.partial(fused, np_, nh), out_shape=(shape((nh, t...  63.5 us
    pallas_call x1, Pallas kernels, on_device(): pl.pallas_call(functools.partial(finish, nh, steps), out_shape=(shape((ki...  3.04 us

profile of v3, /device:TPU:5, one launch (start us, length us, event | category | flops | bytes accessed | tf_op | source)
XLA Modules:
  0.0 67.2 jit_solution(18329184444202518957)
XLA Ops:
  0.6 63.5 %shard_map.202 = (bf16[16,9,16,128]{3,2,1,0:T(8,128)(2,1)}, f32[8,8,64,128]{3,2,1,0:T(8,128)}, f32[3,8,512]{2,1,0:T(8,128)}) custom-call(s32[8]{0:T(128)} %counts_h.1, f32[8]{0:T(128)} %step_bias_h.1, f32[8]{0:T(128)} %decay_log_h.1, f32[8]{0:T(128)} %skip_gain_h.1, s32[4,128]{1,0:T(4,128)} %bitcast.12, f32[4,512]{1,0:T(4,128)} %kern_value_h.1, ...), custom_call_target="tpu_custom_call" | custom-call | tf_op jit(solution)/shard_map/pallas_call | solution.py:913
  64.1 3.0 %shard_map.203 = (bf16[8,4,512]{2,1,0:T(4,128)(2,1)}, f32[8,8,64,128]{3,2,1,0:T(8,128)}, f32[3,8,512]{2,1,0:T(8,128)}) custom-call(bf16[16,9,16,128]{3,2,1,0:T(8,128)(2,1)} %get-tuple-element.9.parts_h, f32[8,8,64,128]{3,2,1,0:T(8,128)} %get-tuple-element.10.states_h, f32[3,8,512]{2,1,0:T(8,128)} %get-tuple-element.11.conv_h), custom_call_target="tpu_custom_call" | custom-call | tf_op jit(solution)/shard_map/pallas_call | solution.py:947

commit v4 on v3

--- a/solution.py
+++ b/solution.py
@@ -1,4 +1,5 @@
 import functools
+import math
 
 import jax
 import jax.numpy as jnp
@@ -14,6 +15,7 @@
 BF16 = jnp.bfloat16
 LANES = 128
 EMB_PIECES = 4
+BATCHES = (((0, 1, 2), 0), ((3, 4), 0), ((5, 6, 7), 1))
 
 
 def silu(x):
@@ -76,7 +78,7 @@
     w_wread,
     w_step,
     w_output,
-    parts_o,
+    mixed_o,
     states_o,
     conv_o,
     counts,
@@ -122,6 +124,7 @@
     quarter,
     nrm_all,
     part,
+    parts,
     fin,
     conv_v,
     tok_sem,
@@ -149,7 +152,6 @@
     fwd_recv,
     out_send,
     out_recv,
-    own_sem,
     res_sem,
 ):
     p = lax.axis_index("particle")
@@ -181,23 +183,6 @@
     def chip(d):
         return lax.rem(z + d + zs, zs)
 
-    barrier = pltpu.get_barrier_semaphore()
-
-    def greet_head(j, _):
-        pl.semaphore_signal(
-            barrier, inc=1, device_id={"head": lax.rem(h + j, nh)}, device_id_type=MESH
-        )
-        return 0
-
-    def greet_particle(j, _):
-        pl.semaphore_signal(
-            barrier, inc=1, device_id={"particle": lax.rem(p + j, np_)}, device_id_type=MESH
-        )
-        return 0
-
-    lax.fori_loop(1, nh, greet_head, 0)
-    lax.fori_loop(1, np_, greet_particle, 0)
-
     tok_copy = pltpu.make_async_copy(tok_h, tok, tok_sem)
     tok_copy.start()
     piece = vocab // EMB_PIECES
@@ -209,6 +194,13 @@
     ]
     for copy in emb_copies:
         copy.start()
+
+    barrier = pltpu.get_barrier_semaphore()
+    mates = [{"head": lax.rem(h + j, nh)} for j in range(1, nh)]
+    mates += [{"particle": lax.rem(p + 2 * j, np_)} for j in range(1, zs)]
+    mates += [{"particle": sibling}, {"particle": lax.rem(p + np_ - 1 + 2 * c, np_)}]
+    for other in mates:
+        pl.semaphore_signal(barrier, inc=1, device_id=other, device_id_type=MESH)
     at_write = pl.ds(pl.multiple_of(group * state, state), state)
     at_read = pl.ds(pl.multiple_of((GROUPS + group) * state, state), state)
     side = mate // (span // 2)
@@ -237,8 +229,6 @@
         (bias_wread.at[:, at_read], bw_v.at[:, hi]),
     ]
     loads = [pltpu.make_async_copy(s, d, loc_sem.at[i]) for i, (s, d) in enumerate(pairs)]
-    for copy in loads:
-        copy.start()
 
     tok_copy.wait()
     ids_t = jnp.concatenate([tok[...], jnp.zeros((8 - steps, np_ * kids), jnp.int32)], axis=0).T
@@ -261,8 +251,19 @@
             total = term if total is None else total + term
         tok_part[m] = total.astype(BF16).reshape(nh, owned, -1)
 
+    side_x = math.isqrt(nh)
+    side_y = nh // side_x
+    offsets = [(a, b) for a in range(side_x) for b in range(side_y) if a or b]
+    offsets.sort(key=lambda o: -min(o[0], side_x - o[0]) - min(o[1], side_y - o[1]))
+
+    def at_offset(j, way):
+        a, b = offsets[j - 1]
+        x = lax.rem(h // side_y + way * a + side_x, side_x)
+        y = lax.rem(h % side_y + way * b + side_y, side_y)
+        return x * side_y + y
+
     def rs_copy(m, j):
-        dest = lax.rem(h + j, nh)
+        dest = at_offset(j, 1)
         return pltpu.make_async_remote_copy(
             src_ref=tok_part.at[m, dest],
             dst_ref=tok_recv.at[m, j - 1],
@@ -278,12 +279,12 @@
             dst_ref=tok_all.at[m, h],
             send_sem=ag_send.at[m, j - 1],
             recv_sem=ag_recv.at[m, j - 1],
-            device_id={"head": lax.rem(h + j, nh)},
+            device_id={"head": at_offset(j, 1)},
             device_id_type=MESH,
         )
 
     def ag_back(m, j):
-        source = lax.rem(h + nh - j, nh)
+        source = at_offset(j, -1)
         return pltpu.make_async_remote_copy(
             src_ref=tok_all.at[m, h],
             dst_ref=tok_all.at[m, source],
@@ -294,15 +295,16 @@
         )
 
     def each(do):
-        def step(j, _):
+        for j in range(1, nh):
             do(j)
-            return 0
-
-        lax.fori_loop(1, nh, step, 0)
 
     lookup(0)
-    pl.semaphore_wait(barrier, nh - 1 + np_ - 1)
+    pl.semaphore_wait(barrier, len(mates))
     each(lambda j: rs_copy(0, j).start())
+    lookup(1)
+    each(lambda j: rs_copy(1, j).start())
+    for copy in loads:
+        copy.start()
 
     above = lax.rem(p + 1, np_)
     shift_pairs = [
@@ -324,8 +326,6 @@
     ]
     for copy in shifts:
         copy.start()
-    lookup(1)
-    each(lambda j: rs_copy(1, j).start())
 
     for m in range(2):
         each(lambda j, m=m: rs_copy(m, j).wait_recv())
@@ -544,20 +544,28 @@
     first = lax.dot_general(
         apart(reads, kids), sbf[...], (((1,), (1,)), ((), ())), preferred_element_type=F32
     )
+    kept = None
+    starts = []
+    for t in range(steps):
+        now = at_step(decay, t)
+        kept = now if kept is None else kept * now
+        starts.append(kept * at_step(first, t))
+    match = {
+        (u, t): jnp.sum(writes[u] * reads[t], axis=1, keepdims=True)
+        for t in range(steps)
+        for u in range(t + 1)
+    }
     value = arrive(1).astype(F32)
     conv = convolve(hist, value, kern_value[...], bias_value[...])
 
-    kept = None
     added = []
     readings = []
     for t in range(steps):
         now = at_step(decay, t)
-        kept = now if kept is None else kept * now
         added = [a * now for a in added] + [at_step(step_size, t) * conv[t]]
-        reading = kept * at_step(first, t) + skip * conv[t]
+        reading = starts[t] + skip * conv[t]
         for u in range(t + 1):
-            match = jnp.sum(writes[u] * reads[t], axis=1, keepdims=True)
-            reading = reading + added[u] * match
+            reading = reading + added[u] * match[u, t]
         readings.append(reading)
     gate = jnp.concatenate([arrive_gate(q) for q in range(2)], axis=0).astype(F32)
     gated = jnp.concatenate(readings, axis=0) * silu(gate)
@@ -626,73 +634,69 @@
     for copy in results:
         copy.start()
 
-    def dest_of(i, core):
-        return lax.rem(z - order[i] + zs, zs) * 2 + core
-
-    def out_copy(i, core):
-        return pltpu.make_async_remote_copy(
-            src_ref=part.at[i, core],
-            dst_ref=parts_o.at[h],
-            send_sem=out_send.at[i, core],
+    def dest_of(i, other):
+        return chip(-order[i]) * 2 + (1 - c if other else c)
+
+    def out_copy(i, other):
+        return pltpu.make_async_remote_copy(
+            src_ref=part.at[i, other],
+            dst_ref=parts.at[h],
+            send_sem=out_send.at[i, other],
             recv_sem=out_recv.at[h],
-            device_id={"head": dest_of(i, core)},
-            device_id_type=MESH,
-        )
-
-    def own_copy(i, core):
-        return pltpu.make_async_copy(part.at[i, core], parts_o.at[h], own_sem)
+            device_id={"head": dest_of(i, other)},
+            device_id_type=MESH,
+        )
 
     def send_parts(places):
         block = []
-        for i in places:
-            for core in range(2):
-                tiles = nrm_all[dest_of(i, core)]
-                for r in range(bands):
-                    block.append(
-                        jnp.concatenate([tiles[r * cuts + n] for n in range(cuts)], axis=1)
-                    )
+        for i, other in places:
+            tiles = nrm_all[dest_of(i, other)]
+            for r in range(bands):
+                block.append(
+                    jnp.concatenate([tiles[r * cuts + n] for n in range(cuts)], axis=1)
+                )
         product = jnp.dot(
             jnp.concatenate(block, axis=0), wo_v[...], preferred_element_type=F32
         ).astype(BF16)
-        for n, i in enumerate(places):
-            for core in range(2):
-                for r in range(bands):
-                    start = (2 * n + core) * own + r * 16
-                    for e in range(cuts):
-                        part[i, core, r * cuts + e] = product[
-                            start : start + 16, e * LANES : (e + 1) * LANES
-                        ]
-                part[i, core, bands * cuts] = nrm_all[dest_of(i, core), bands * cuts]
-        for i in places:
-            for core in range(2):
-                dest = dest_of(i, core)
-
-                @pl.when(dest != h)
-                def _(i=i, core=core):
-                    out_copy(i, core).start()
-
-                @pl.when(dest == h)
-                def _(i=i, core=core):
-                    own_copy(i, core).start()
+        for n, (i, other) in enumerate(places):
+            for r in range(bands):
+                start = n * own + r * 16
+                for e in range(cuts):
+                    part[i, other, r * cuts + e] = product[
+                        start : start + 16, e * LANES : (e + 1) * LANES
+                    ]
+            part[i, other, bands * cuts] = nrm_all[dest_of(i, other), bands * cuts]
+        for i, other in places:
+            dest = dest_of(i, other)
+
+            @pl.when(dest != h)
+            def _(i=i, other=other):
+                out_copy(i, other).start()
+
+            @pl.when(dest == h)
+            def _(i=i, other=other):
+                parts[h] = part[i, other]
 
     def take(i):
-        at = lax.rem(p - 2 * order[i] + np_, np_)
+        at = chip(-order[i]) * 2 + c
         if order[i] != 0:
             nrm_copy(at, sibling, nrm_send.at[i], nrm_recv.at[i]).wait_recv()
             forward(i).start()
 
     def take_forward(i):
-        at = lax.rem(sibling - 2 * order[i] + np_, np_)
+        at = chip(-order[i]) * 2 + 1 - c
         nrm_copy(at, sibling, fwd_send.at[i], fwd_recv.at[i]).wait_recv()
 
     near = list(range(zs))[::-1]
-    batches = [near[:3], near[3:5], near[5:]]
-    for batch in batches:
+    for batch, split in BATCHES:
+        batch = [near[n] for n in batch]
         for i in batch:
             take(i)
+        if split:
+            send_parts([(i, 0) for i in batch])
         for i in batch:
             take_forward(i)
-        send_parts(batch)
+        send_parts([(i, o) for i in batch for o in range(split, 2)])
 
     for m in range(2):
         each(lambda j, m=m: rs_copy(m, j).wait_send())
@@ -717,82 +721,52 @@
         forward(i).wait_send()
     for copy in results:
         copy.wait()
+
+    totals = [[jnp.zeros((16, LANES), F32) for _ in range(cuts)] for _ in range(bands)]
+    for g in range(GROUPS):
+        sums = [[jnp.zeros((16, LANES), F32) for _ in range(cuts)] for _ in range(bands)]
+        squares = [jnp.zeros((16, 1), F32) for _ in range(bands)]
+        for s in range(g * span, (g + 1) * span):
+
+            @pl.when(s != h)
+            def _(s=s):
+                pltpu.make_async_remote_copy(
+                    src_ref=part.at[0, 0],
+                    dst_ref=parts.at[s],
+                    send_sem=out_send.at[0, 0],
+                    recv_sem=out_recv.at[s],
+                    device_id={"head": s},
+                    device_id_type=MESH,
+                ).wait_recv()
+
+            marks = parts[s, bands * cuts].astype(F32)
+            for r in range(bands):
+                squares[r] = squares[r] + marks[:, 2 * r : 2 * r + 1] + marks[:, 2 * r + 1 : 2 * r + 2]
+                for e in range(cuts):
+                    sums[r][e] = sums[r][e] + parts[s, r * cuts + e].astype(F32)
+        for r in range(bands):
+            scale = lax.rsqrt(squares[r] / (width * span) + EPSILON)
+            totals[r] = [a + b * scale for a, b in zip(totals[r], sums[r])]
+    for r in range(bands):
+        answer = jnp.concatenate(totals[r], axis=1)
+        each_kid = 16 // steps
+        for k in range(each_kid):
+            mixed_o[r * each_kid + k] = answer[k * steps : (k + 1) * steps].astype(BF16)
     for i in range(zs):
-        for core in range(2):
-            dest = dest_of(i, core)
-
-            @pl.when(dest != h)
-            def _(i=i, core=core):
-                out_copy(i, core).wait_send()
-
-    own_copy(0, 0).wait()
-
-    def out_wait(s, _):
-        @pl.when(s != h)
-        def _():
-            pltpu.make_async_remote_copy(
-                src_ref=part.at[0, 0],
-                dst_ref=parts_o.at[s],
-                send_sem=out_send.at[0, 0],
-                recv_sem=out_recv.at[s],
-                device_id={"head": s},
-                device_id_type=MESH,
-            ).wait_recv()
-
-        return 0
-
-    lax.fori_loop(0, nh, out_wait, 0)
-
-
-def finish(
-    nh,
-    steps,
-    parts_h,
-    states_h,
-    conv_h,
-    mixed,
-    final_state,
-    final_conv,
-    parts,
-    states,
-    conv,
-    in_sems,
-    out_sems,
-):
-    kids, heads, headdim, _ = states_h.shape
-    width = heads * headdim
-    span = nh // GROUPS
-    load = pltpu.make_async_copy(parts_h, parts, in_sems.at[kids + 1])
-    pairs = [(states_h.at[k], states.at[k], final_state.at[k]) for k in range(kids)]
-    pairs.append((conv_h, conv, final_conv))
-    pulls = [pltpu.make_async_copy(a, b, in_sems.at[i]) for i, (a, b, _) in enumerate(pairs)]
-    pushes = [pltpu.make_async_copy(b, d, out_sems.at[i]) for i, (_, b, d) in enumerate(pairs)]
-    for copy in pulls:
+        for other in range(2):
+
+            @pl.when(dest_of(i, other) != h)
+            def _(i=i, other=other):
+                out_copy(i, other).wait_send()
+
+
+def finish(mixed, states, conv, mixed_o, states_o, conv_o, sems):
+    pairs = [(states.at[k], states_o.at[k]) for k in range(states.shape[0])]
+    pairs += [(mixed, mixed_o), (conv, conv_o)]
+    copies = [pltpu.make_async_copy(a, b, sems.at[i]) for i, (a, b) in enumerate(pairs)]
+    for copy in copies:
         copy.start()
-    load.start()
-    for pull, push in zip(pulls, pushes):
-        pull.wait()
-        push.start()
-    load.wait()
-    cuts = mixed.shape[2] // LANES
-    bands = (parts.shape[1] - 1) // cuts
-    for r in range(bands):
-        answer = [jnp.zeros((16, LANES), F32) for _ in range(cuts)]
-        for g in range(GROUPS):
-            square = jnp.zeros((16, 1), F32)
-            total = [jnp.zeros((16, LANES), F32) for _ in range(cuts)]
-            for s in range(g * span, (g + 1) * span):
-                mark = parts[s, bands * cuts].astype(F32)[:, 2 * r : 2 * r + 2]
-                square = square + mark[:, 0:1] + mark[:, 1:2]
-                for i in range(cuts):
-                    total[i] = total[i] + parts[s, r * cuts + i].astype(F32)
-            scale = lax.rsqrt(square / (width * span) + EPSILON)
-            answer = [a + b * scale for a, b in zip(answer, total)]
-        answer = jnp.concatenate(answer, axis=1)
-        each = 16 // steps
-        for k in range(each):
-            mixed[r * each + k] = answer[k * steps : (k + 1) * steps].astype(BF16)
-    for copy in pushes:
+    for copy in copies:
         copy.wait()
 
 
@@ -877,6 +851,7 @@
         vmem((span, own, LANES), BF16),
         vmem((np_, tiles, 16, LANES), BF16),
         vmem((zs, 2, tiles, 16, LANES), BF16),
+        vmem((nh, tiles, 16, LANES), BF16),
         vmem(ssm_state.shape, F32),
         vmem((3, kids, width), F32),
         dma,
@@ -904,27 +879,12 @@
         dma((zs,)),
         dma((zs, 2)),
         dma((nh,)),
-        dma,
         dma((2,)),
     ]
     hbm = pl.BlockSpec(memory_space=pltpu.HBM)
-    limit = 60 * 1024 * 1024
+    limit = 40 * 1024 * 1024
     shape = jax.ShapeDtypeStruct
-    parts, states, conv = pl.pallas_call(
-        functools.partial(fused, np_, nh),
-        out_shape=(
-            shape((nh, tiles, 16, LANES), BF16),
-            shape(ssm_state.shape, F32),
-            shape((3, kids, width), F32),
-        ),
-        in_specs=[hbm] * 19,
-        out_specs=(hbm,) * 3,
-        scratch_shapes=scratch,
-        compiler_params=pltpu.CompilerParams(
-            collective_id=0, has_side_effects=True, vmem_limit_bytes=limit
-        ),
-    )(
-        counts,
+    operands = (        counts,
         step_bias,
         decay_log,
         skip_gain,
@@ -944,24 +904,34 @@
         w_step.T,
         w_output,
     )
-    mixed, final_state, final_conv = pl.pallas_call(
-        functools.partial(finish, nh, steps),
+    operands = [pltpu.with_memory_space_constraint(a, pltpu.HBM) for a in operands]
+    results = pl.pallas_call(
+        functools.partial(fused, np_, nh),
         out_shape=(
             shape((kids, steps, cols), BF16),
             shape(ssm_state.shape, F32),
             shape((3, kids, width), F32),
         ),
-        in_specs=[hbm] * 3,
-        out_specs=(pl.BlockSpec(memory_space=pltpu.VMEM), hbm, hbm),
-        scratch_shapes=[
-            vmem((nh, tiles, 16, LANES), BF16),
-            vmem(ssm_state.shape, F32),
-            vmem((3, kids, width), F32),
-            dma((kids + 2,)),
-            dma((kids + 1,)),
-        ],
+        in_specs=[hbm] * 19,
+        out_specs=(pl.BlockSpec(memory_space=pltpu.VMEM),)
+        + (pl.BlockSpec(memory_space=pl.ANY),) * 2,
+        scratch_shapes=scratch,
+        compiler_params=pltpu.CompilerParams(
+            collective_id=0, has_side_effects=True, vmem_limit_bytes=limit
+        ),
+    )(*operands)
+    mixed, final_state, final_conv = pl.pallas_call(
+        finish,
+        out_shape=(
+            shape((kids, steps, cols), BF16),
+            shape(ssm_state.shape, F32),
+            shape((3, kids, width), F32),
+        ),
+        in_specs=[pl.BlockSpec(memory_space=pltpu.VMEM)] * 3,
+        out_specs=(hbm,) * 3,
+        scratch_shapes=[dma((kids + 2,))],
         compiler_params=pltpu.CompilerParams(vmem_limit_bytes=limit),
-    )(parts, states, conv)
+    )(*results)
     return mixed, final_state, final_conv.transpose(1, 0, 2)
 
 

time: 67.3 us -> 62.8 us (0.933)
  Pallas kernels: 66.5 us -> 62.1 us
    pallas_call x2, Pallas kernels: 66.5 us -> 62.1 us  [the longest x1 60.6 us: on_device(): pl.pallas_call(functools.partial(fused, np_, nh), out_shape=(shape((kids,...]
where the time goes in v4:
time: 62.8 us; the launch traced here: 62.7 us
  Pallas kernels  62.1 us (99%)
  between operations  0.65 us (1%)
    pallas_call x1, Pallas kernels, on_device(): pl.pallas_call(functools.partial(fused, np_, nh), out_shape=(shape((kids,...  60.6 us
    pallas_call x1, Pallas kernels, on_device(): pl.pallas_call(finish, out_shape=(shape((kids, steps, cols), BF16), shape...  1.41 us

profile of v4, /device:TPU:5, one launch (start us, length us, event | category | flops | bytes accessed | tf_op | source)
XLA Modules:
  0.0 62.7 jit_solution(10983506013882693304)
XLA Ops:
  0.6 60.6 %shard_map.202 = (bf16[8,4,512]{2,1,0:T(4,128)(2,1)S(1)}, f32[8,8,64,128]{3,2,1,0:T(8,128)S(1)}, f32[3,8,512]{2,1,0:T(8,128)S(1)}) custom-call(s32[8]{0:T(128)} %counts_h.1, f32[8]{0:T(128)} %step_bias_h.1, f32[8]{0:T(128)} %decay_log_h.1, f32[8]{0:T(128)} %skip_gain_h.1, s32[4,128]{1,0:T(4,128)} %bitcast.12, f32[4,512]{1,0:T(4,128)} %kern_value_h.1, ...), custom_call_target="tpu_custom_call" | custom-call | tf_op jit(solution)/shard_map/pallas_call | solution.py:908
  61.3 1.4 %shard_map.203 = (bf16[8,4,512]{2,1,0:T(4,128)(2,1)}, f32[8,8,64,128]{3,2,1,0:T(8,128)}, f32[3,8,512]{2,1,0:T(8,128)}) custom-call(bf16[8,4,512]{2,1,0:T(4,128)(2,1)S(1)} %get-tuple-element.9.mixed, f32[8,8,64,128]{3,2,1,0:T(8,128)S(1)} %get-tuple-element.10.states, f32[3,8,512]{2,1,0:T(8,128)S(1)} %get-tuple-element.11.conv), custom_call_target="tpu_custom_call" | custom-call | tf_op jit(solution)/shard_map/pallas_call | solution.py:923

commit v5 on v4

--- a/solution.py
+++ b/solution.py
@@ -438,6 +438,7 @@
     for m in range(2):
         each(lambda j, m=m: ag_back(m, j).wait_recv())
         tokens = tok_all[m].reshape(half, -1)
+        place(2, m, jnp.dot(tokens, wg_v[...], preferred_element_type=F32))
         matrices = jnp.dot(tokens, ww_v[...], preferred_element_type=F32)
         rate = lax.dot_general(
             tokens, ws_v[...], (((1,), (1,)), ((), ())), preferred_element_type=F32
@@ -447,10 +448,6 @@
         turned = jnp.concatenate([matrices[:, share:], matrices[:, :share]], axis=1)
         matrices = jnp.where(mate % (span // 2) == 0, matrices, turned)
         place(0, m, jnp.where(iota((half, LANES), 1) < share, matrices, rate))
-        place(2, m, jnp.dot(tokens, wg_v[...], preferred_element_type=F32))
-        place(1, m, jnp.dot(tokens, wv_v[...], preferred_element_type=F32))
-        sib_copy(0, m).wait_recv()
-        send_sums(0, range(m * reach, min((m + 1) * reach, zs - 1)))
         sib_copy(2, m).wait_recv()
         if m == 0:
             for q, way in legs:
@@ -459,8 +456,11 @@
                     out_far[q, side, 0] = gate_sum(reach, q).astype(BF16)
                 out_far[q, side, 1] = gate_sum(way * (reach - 1), q).astype(BF16)
                 far_copy(q, way).start()
+        place(1, m, jnp.dot(tokens, wv_v[...], preferred_element_type=F32))
+        sib_copy(0, m).wait_recv()
+        send_sums(0, range(m * reach, min((m + 1) * reach, zs - 1)))
         sib_copy(1, m).wait_recv()
-        send_sums(1, range(1) if m == 0 else range(1, zs - 1))
+    send_sums(1, range(zs - 1))
     for q, way in legs:
         side = (1 - way) // 2
         far_copy(q, way).wait_recv()
@@ -570,23 +570,15 @@
     gate = jnp.concatenate([arrive_gate(q) for q in range(2)], axis=0).astype(F32)
     gated = jnp.concatenate(readings, axis=0) * silu(gate)
 
-    squares = jnp.sum(gated * gated, axis=1, keepdims=True)
-    upper = squares.astype(BF16).astype(F32)
-    lane = iota((own, LANES), 1)
-    squares = jnp.where(lane % 2 == 0, upper, squares - upper).astype(BF16)
-    scaled = jnp.concatenate([(gated * norm_gain[...]).astype(BF16), squares], axis=1)
+    scaled = (gated * norm_gain[...]).astype(BF16)
     at_row, from_row = iota((own, own), 0), iota((own, own), 1)
     turn = (from_row == (at_row % steps) * kids + at_row // steps).astype(F32).astype(BF16)
     scaled = jnp.dot(turn, scaled, preferred_element_type=F32)
     bands, cuts = own // 16, width // LANES
-    marks = scaled[:16, width:]
     for r in range(bands):
-        band = scaled[r * 16 : (r + 1) * 16]
         for i in range(cuts):
-            nrm_all[p, r * cuts + i] = band[:, i * LANES : (i + 1) * LANES].astype(BF16)
-        if r > 0:
-            marks = jnp.where(iota(marks.shape, 1) < 2 * r, marks, band[:, width:])
-    nrm_all[p, bands * cuts] = marks.astype(BF16)
+            tile = scaled[r * 16 : (r + 1) * 16, i * LANES : (i + 1) * LANES]
+            nrm_all[p, r * cuts + i] = tile.astype(BF16)
 
     def nrm_copy(at, target, send, recv):
         return pltpu.make_async_remote_copy(
@@ -655,17 +647,25 @@
                 block.append(
                     jnp.concatenate([tiles[r * cuts + n] for n in range(cuts)], axis=1)
                 )
-        product = jnp.dot(
-            jnp.concatenate(block, axis=0), wo_v[...], preferred_element_type=F32
-        ).astype(BF16)
+        block = jnp.concatenate(block, axis=0)
+        product = jnp.dot(block, wo_v[...], preferred_element_type=F32).astype(BF16)
+        plain = block.astype(F32) * ungain
+        squares = jnp.sum(plain * plain, axis=1, keepdims=True)
+        upper = squares.astype(BF16).astype(F32)
+        lane = iota((block.shape[0], LANES), 1)
+        squares = jnp.where(lane % 2 == 0, upper, squares - upper)
         for n, (i, other) in enumerate(places):
+            marks = squares[n * own : n * own + 16]
+            for r in range(1, bands):
+                start = n * own + r * 16
+                marks = jnp.where(lane[:16] < 2 * r, marks, squares[start : start + 16])
+            part[i, other, bands * cuts] = marks.astype(BF16)
             for r in range(bands):
                 start = n * own + r * 16
                 for e in range(cuts):
                     part[i, other, r * cuts + e] = product[
                         start : start + 16, e * LANES : (e + 1) * LANES
                     ]
-            part[i, other, bands * cuts] = nrm_all[dest_of(i, other), bands * cuts]
         for i, other in places:
             dest = dest_of(i, other)
 
@@ -687,6 +687,7 @@
         at = chip(-order[i]) * 2 + 1 - c
         nrm_copy(at, sibling, fwd_send.at[i], fwd_recv.at[i]).wait_recv()
 
+    ungain = 1.0 / norm_gain[...]
     near = list(range(zs))[::-1]
     for batch, split in BATCHES:
         batch = [near[n] for n in batch]
@@ -849,7 +850,7 @@
         vmem((2, 2, 2, own // 2, width), BF16),
         vmem((2, 2, 2, own // 2, width), BF16),
         vmem((span, own, LANES), BF16),
-        vmem((np_, tiles, 16, LANES), BF16),
+        vmem((np_, tiles - 1, 16, LANES), BF16),
         vmem((zs, 2, tiles, 16, LANES), BF16),
         vmem((nh, tiles, 16, LANES), BF16),
         vmem(ssm_state.shape, F32),

time: 62.8 us -> 61.3 us (0.976)
  Pallas kernels: 62.1 us -> 60.5 us
    pallas_call x1, Pallas kernels: 60.6 us -> 59.1 us  [on_device(): pl.pallas_call(functools.partial(fused, np_, nh), out_shape=(shape((kids,...]
where the time goes in v5:
time: 61.3 us; the launch traced here: 61.2 us
  Pallas kernels  60.5 us (99%)
  between operations  0.65 us (1%)
    pallas_call x1, Pallas kernels, on_device(): pl.pallas_call(functools.partial(fused, np_, nh), out_shape=(shape((kids,...  59.1 us
    pallas_call x1, Pallas kernels, on_device(): pl.pallas_call(finish, out_shape=(shape((kids, steps, cols), BF16), shape...  1.41 us

profile of v5, /device:TPU:5, one launch (start us, length us, event | category | flops | bytes accessed | tf_op | source)
XLA Modules:
  0.0 61.2 jit_solution(15958275612922509762)
XLA Ops:
  0.6 59.1 %shard_map.202 = (bf16[8,4,512]{2,1,0:T(4,128)(2,1)S(1)}, f32[8,8,64,128]{3,2,1,0:T(8,128)S(1)}, f32[3,8,512]{2,1,0:T(8,128)S(1)}) custom-call(s32[8]{0:T(128)} %counts_h.1, f32[8]{0:T(128)} %step_bias_h.1, f32[8]{0:T(128)} %decay_log_h.1, f32[8]{0:T(128)} %skip_gain_h.1, s32[4,128]{1,0:T(4,128)} %bitcast.12, f32[4,512]{1,0:T(4,128)} %kern_value_h.1, ...), custom_call_target="tpu_custom_call" | custom-call | tf_op jit(solution)/shard_map/pallas_call | solution.py:909
  59.8 1.4 %shard_map.203 = (bf16[8,4,512]{2,1,0:T(4,128)(2,1)}, f32[8,8,64,128]{3,2,1,0:T(8,128)}, f32[3,8,512]{2,1,0:T(8,128)}) custom-call(bf16[8,4,512]{2,1,0:T(4,128)(2,1)S(1)} %get-tuple-element.9.mixed, f32[8,8,64,128]{3,2,1,0:T(8,128)S(1)} %get-tuple-element.10.states, f32[3,8,512]{2,1,0:T(8,128)S(1)} %get-tuple-element.11.conv), custom_call_target="tpu_custom_call" | custom-call | tf_op jit(solution)/shard_map/pallas_call | solution.py:924

commit v6 on v5

--- a/solution.py
+++ b/solution.py
@@ -328,10 +328,10 @@
         copy.start()
 
     for m in range(2):
-        each(lambda j, m=m: rs_copy(m, j).wait_recv())
         shared = tok_part[m, h]
-        for s in range(nh - 1):
-            shared = shared + tok_recv[m, s]
+        for j in reversed(range(1, nh)):
+            rs_copy(m, j).wait_recv()
+            shared = shared + tok_recv[m, j - 1]
         tok_all[m, h] = shared
         each(lambda j, m=m: ag_copy(m, j).start())
 
@@ -601,30 +601,6 @@
     for i in reversed(range(zs - 1)):
         direct(i).start()
     forward(zs - 1).start()
-
-    adds = lax.dot_general(
-        jnp.concatenate(added, axis=0).astype(BF16),
-        apart(writes, kids),
-        (((0,), (0,)), ((), ())),
-        preferred_element_type=F32,
-    )
-    for k in range(kids):
-        for i in range(heads):
-            factor = jnp.broadcast_to(
-                kept[k : k + 1, i * headdim : i * headdim + 1], (headdim, state)
-            )
-            fin[k, i] = (
-                win[parent[k], i] * factor
-                + adds[i * headdim : (i + 1) * headdim, k * state : (k + 1) * state]
-            )
-    for i in range(3):
-        conv_v[i] = at_step(value, steps - 3 + i)
-    results = [
-        pltpu.make_async_copy(s, d, res_sem.at[i])
-        for i, (s, d) in enumerate([(fin, states_o), (conv_v, conv_o)])
-    ]
-    for copy in results:
-        copy.start()
 
     def dest_of(i, other):
         return chip(-order[i]) * 2 + (1 - c if other else c)
@@ -698,6 +674,30 @@
         for i in batch:
             take_forward(i)
         send_parts([(i, o) for i in batch for o in range(split, 2)])
+
+    adds = lax.dot_general(
+        jnp.concatenate(added, axis=0).astype(BF16),
+        apart(writes, kids),
+        (((0,), (0,)), ((), ())),
+        preferred_element_type=F32,
+    )
+    for k in range(kids):
+        for i in range(heads):
+            factor = jnp.broadcast_to(
+                kept[k : k + 1, i * headdim : i * headdim + 1], (headdim, state)
+            )
+            fin[k, i] = (
+                win[parent[k], i] * factor
+                + adds[i * headdim : (i + 1) * headdim, k * state : (k + 1) * state]
+            )
+    for i in range(3):
+        conv_v[i] = at_step(value, steps - 3 + i)
+    results = [
+        pltpu.make_async_copy(s, d, res_sem.at[i])
+        for i, (s, d) in enumerate([(fin, states_o), (conv_v, conv_o)])
+    ]
+    for copy in results:
+        copy.start()
 
     for m in range(2):
         each(lambda j, m=m: rs_copy(m, j).wait_send())

time: 61.3 us -> 61.5 us (level)
  no operation moved by 1% of the time
where the time goes in v6:
time: 61.5 us; the launch traced here: 61.1 us
  Pallas kernels  60.5 us (98%)
  between operations  0.65 us (1%)
    pallas_call x1, Pallas kernels, on_device(): pl.pallas_call(functools.partial(fused, np_, nh), out_shape=(shape((kids,...  59.1 us
    pallas_call x1, Pallas kernels, on_device(): pl.pallas_call(finish, out_shape=(shape((kids, steps, cols), BF16), shape...  1.41 us

profile of v6, /device:TPU:5, one launch (start us, length us, event | category | flops | bytes accessed | tf_op | source)
XLA Modules:
  0.0 61.1 jit_solution(7389285969197414398)
XLA Ops:
  0.6 59.1 %shard_map.202 = (bf16[8,4,512]{2,1,0:T(4,128)(2,1)S(1)}, f32[8,8,64,128]{3,2,1,0:T(8,128)S(1)}, f32[3,8,512]{2,1,0:T(8,128)S(1)}) custom-call(s32[8]{0:T(128)} %counts_h.1, f32[8]{0:T(128)} %step_bias_h.1, f32[8]{0:T(128)} %decay_log_h.1, f32[8]{0:T(128)} %skip_gain_h.1, s32[4,128]{1,0:T(4,128)} %bitcast.12, f32[4,512]{1,0:T(4,128)} %kern_value_h.1, ...), custom_call_target="tpu_custom_call" | custom-call | tf_op jit(solution)/shard_map/pallas_call | solution.py:909
  59.7 1.4 %shard_map.203 = (bf16[8,4,512]{2,1,0:T(4,128)(2,1)}, f32[8,8,64,128]{3,2,1,0:T(8,128)}, f32[3,8,512]{2,1,0:T(8,128)}) custom-call(bf16[8,4,512]{2,1,0:T(4,128)(2,1)S(1)} %get-tuple-element.9.mixed, f32[8,8,64,128]{3,2,1,0:T(8,128)S(1)} %get-tuple-element.10.states, f32[3,8,512]{2,1,0:T(8,128)S(1)} %get-tuple-element.11.conv), custom_call_target="tpu_custom_call" | custom-call | tf_op jit(solution)/shard_map/pallas_call | solution.py:924
